TPU v7x, 512 devices: a whole 4x4x16 slice. The times are simulated.
512 devices in a mesh: gx: 32 (over y, x, core), gy: 16 (over z).
Axes of the slice: x: 4, y: 4, z: 16, core: 2. Of those that a mesh axis runs over, the one named last changes fastest.
Arguments:
- right_side: float32 [3, 512, 256, 512], P(None, 'gx', 'gy'), may hold values from -8 to 8
- viscosity: float32 [512, 256, 512], P('gx', 'gy'), may hold values from 0.05 to 20
- reaction: float32 [512, 256, 512], P('gx', 'gy'), may hold values from 0.5 to 4
- agg_ids: int32 [512, 256, 512], P('gx', 'gy'), may hold values from 0 to 511
- owner_map: int32 [32, 16], P('gx', 'gy'), may hold values from 0 to 31, as said below
Outputs:
- velocity: float32 [3, 512, 256, 512], P(None, 'gx', 'gy')
- corrections: float32 [32, 16, 4, 3, 512], P('gx', 'gy')
Inputs may be any that keep to these rules, and one draw needn't show every extreme that they name: `owner_map`: in every column along gy exactly one owner takes the blocks of 4 devices, its own among them; 3 devices own no block; every other device owns its own block.
All inputs are finite; a program needn't handle non-finite values.
Results may differ from a plain program's by a relative error of at most 0.0003.
Values sent between devices are 32-bit elements; how exact they have to be, the bound alone decides.
No kernel may reach another device: no remote copies, remote signals or barrier semaphores. Data moves between devices by JAX's collectives and lax.ppermute only.
A program may use at most 64 MiB of HBM per device.

v0:
```python
import math

import jax
import jax.numpy as jnp
from jax import lax
from jax.sharding import PartitionSpec as P

COMP = 3
NAGG = 512
NU = 3
MERGES = 3


def padded(block, sides, width):
    for axis, dim in sides:
        count = lax.axis_size(axis)
        forward = [(i, i + 1) for i in range(count - 1)]
        backward = [(target, source) for source, target in forward]
        low = lax.ppermute(
            lax.slice_in_dim(block, block.shape[dim] - width, None, axis=dim), axis, forward
        )
        high = lax.ppermute(lax.slice_in_dim(block, 0, width, axis=dim), axis, backward)
        block = jnp.concatenate([low, block, high], axis=dim)
    return block


def swapped(value, axis, apart):
    mask = 2**apart
    pairs = [(source, source ^ mask) for source in range(lax.axis_size(axis))]
    return lax.ppermute(value, axis, pairs)


def coarse_apply(vector, coarse_diag):
    coupling = 0.2 * jnp.minimum(coarse_diag[..., :-1], coarse_diag[..., 1:])
    coupling = jnp.expand_dims(coupling, -2)
    zeros_end = jnp.zeros_like(vector[..., :1])
    upper = jnp.concatenate([coupling * vector[..., 1:], zeros_end], axis=-1)
    lower = jnp.concatenate([zeros_end, coupling * vector[..., :-1]], axis=-1)
    return jnp.expand_dims(coarse_diag, -2) * vector - (upper + lower)


def smooth_coarse(resid, coarse_diag):
    scaled = jnp.expand_dims(coarse_diag, -2)
    correction = 0.8 * resid / scaled
    correction = correction + 0.8 * (resid - coarse_apply(correction, coarse_diag)) / scaled
    return (correction, resid - coarse_apply(correction, coarse_diag))


def fine_image(velocity, weights, diagonal):
    rimmed = padded(velocity, (("gx", 1), ("gy", 2)), 1)
    padded_vel = jnp.pad(rimmed, ((0, 0), (0, 0), (0, 0), (1, 1)))
    beside = (
        weights[0] * padded_vel[:, 2:, 1:-1, 1:-1] + weights[1] * padded_vel[:, :-2, 1:-1, 1:-1]
    )
    beside = (
        beside
        + weights[2] * padded_vel[:, 1:-1, 2:, 1:-1]
        + weights[3] * padded_vel[:, 1:-1, :-2, 1:-1]
    )
    beside = (
        beside
        + weights[4] * padded_vel[:, 1:-1, 1:-1, 2:]
        + weights[5] * padded_vel[:, 1:-1, 1:-1, :-2]
    )
    return diagonal * velocity - beside


def aggregate_sums(stacked, flat_ids, num_aggs):
    rows, cells = stacked.shape
    block = math.gcd(cells, 2048)
    count = cells // block
    group = math.gcd(count, 8)
    steps = count // group
    value_blocks = stacked.reshape(rows, steps, group, block).transpose(1, 2, 0, 3)
    id_blocks = flat_ids.reshape(steps, group, block)
    labels = jnp.arange(num_aggs, dtype=jnp.int32)

    def add_block(total, pieces):
        values, ids = pieces
        table = (labels[None, :, None] == ids[:, None, :]).astype(jnp.float32)
        part_sums = jnp.einsum("grk,gak->ra", values, table, precision=lax.Precision.HIGHEST)
        return (total + part_sums, None)

    start = jnp.zeros((rows, num_aggs), jnp.float32)
    total, unused = lax.scan(add_block, start, (value_blocks, id_blocks))
    return total


def shards(right_side, viscosity, reaction, agg_ids, owner_map):
    rimmed_visc = padded(viscosity, (("gx", 0), ("gy", 1)), 1)
    padded_visc = jnp.pad(rimmed_visc, ((0, 0), (0, 0), (1, 1)))
    shifted = [
        padded_visc[2:, 1:-1, 1:-1],
        padded_visc[:-2, 1:-1, 1:-1],
        padded_visc[1:-1, 2:, 1:-1],
        padded_visc[1:-1, :-2, 1:-1],
        padded_visc[1:-1, 1:-1, 2:],
        padded_visc[1:-1, 1:-1, :-2],
    ]
    weights = [0.5 * (viscosity + other) for other in shifted]
    diagonal = (
        reaction + weights[0] + weights[1] + weights[2] + weights[3] + weights[4] + weights[5]
    )
    velocity = jnp.zeros_like(right_side)
    for sweep in range(NU):
        image = fine_image(velocity, weights, diagonal)
        velocity = velocity + 0.8 * (right_side - image) / diagonal
    resid = right_side - fine_image(velocity, weights, diagonal)
    stacked = jnp.concatenate([resid, diagonal[None]], axis=0).reshape(COMP + 1, -1)
    block_sums = aggregate_sums(stacked, agg_ids.reshape(-1), NAGG)
    width_gx = lax.axis_size("gx")
    one_hot = (owner_map.reshape(()) == jnp.arange(width_gx, dtype=jnp.int32)).astype(jnp.float32)
    outgoing = one_hot[:, None, None] * block_sums[None]
    arrived = lax.all_to_all(outgoing, "gx", split_axis=0, concat_axis=0, tiled=True)
    owned = jnp.sum(arrived, axis=0)
    coarse_res = owned[:COMP]
    coarse_diag = 1.0 + owned[COMP]
    outputs = []
    for level in range(MERGES + 1):
        correction, left_over = smooth_coarse(coarse_res, coarse_diag)
        outputs.append(correction)
        if level < MERGES:
            other_res, other_diag = swapped((left_over, coarse_diag), "gx", level)
            coarse_res = left_over + other_res
            coarse_diag = coarse_diag + other_diag
    levels_out = jnp.stack(outputs, axis=0)
    return (velocity, levels_out[None, None])


def solution(mesh):
    return jax.shard_map(
        shards,
        mesh=mesh,
        in_specs=(
            P(None, "gx", "gy", None),
            P("gx", "gy", None),
            P("gx", "gy", None),
            P("gx", "gy", None),
            P("gx", "gy"),
        ),
        out_specs=(P(None, "gx", "gy", None), P("gx", "gy", None, None, None)),
        check_vma=False,
    )
```

profile of v0, /device:TPU:480, one launch (start us, length us, event | category | flops | bytes accessed | tf_op | source)
XLA Modules:
  0.0 311.1 jit_solution(2000282416725182054)
XLA Ops:
  1.4 1.7 collective-permute-start.1
  3.1 1.3 collective-permute-start
  4.5 1.1 constant_dynamic-update-slice_fusion.1
  5.6 2.0 collective-permute-done
  7.6 2.9 collective-permute-start.2
  10.5 1.3 collective-permute-start.3
  11.8 1.3 collective-permute-start.4
  13.1 4.9 %collective-permute-start.5 = (f32[3,1,16,512]{3,2,1,0:T(8,128)S(1)}, f32[3,1,16,512]{3,2,1,0:T(8,128)S(1)}, u32[]{:S(2)}, u32[]{:S(2)}) collective-permute-start(f32[3,1,16,512]{3,2,1,0:T(8,128)S(1)} %broadcast.87), channel_id=1, source_target_pairs={{0,16},{16,32},{32,48},{48,64},{64,80},{80,96},{96,112},{112,128},... | collective-permute-start | bytes 294920 | tf_op jit(solution)/shard_map/ppermute | solution.py:19
  19.4 4.4 %collective-permute-start.6 = (f32[3,18,1,512]{3,1,2,0:T(8,128)S(1)}, f32[3,18,1,512]{3,1,2,0:T(8,128)S(1)}, u32[]{:S(2)}, u32[]{:S(2)}) collective-permute-start(f32[3,18,1,512]{3,1,2,0:T(8,128)S(1)} %copy.99), channel_id=1, source_target_pairs={{1,0},{2,1},{3,2},{4,3},{5,4},{6,5},{7,6},{8,7},{9,8},{10,9},{11,1... | collective-permute-start | bytes 331784 | tf_op jit(solution)/shard_map/ppermute | solution.py:22
  23.8 1.3 collective-permute-start.7
  26.6 4.7 %collective-permute-done.7 = f32[3,18,1,512]{3,1,2,0:T(8,128)S(1)} collective-permute-done((f32[3,18,1,512]{3,1,2,0:T(8,128)S(1)}, f32[3,18,1,512]{3,1,2,0:T(8,128)S(1)}, u32[]{:S(2)}, u32[]{:S(2)}) %collective-permute-start.7) | collective-permute-done | bytes 110624 | tf_op jit(solution)/shard_map/ppermute | solution.py:19
  31.4 3.4 %select_maximum_fusion.12 = f32[3,18,18,514]{3,2,1,0:T(8,128)S(1)} fusion(f32[3,18,1,512]{3,2,1,0:T(1,128)S(1)} %copy.100, f32[3,18,1,512]{3,2,1,0:T(1,128)S(1)} %copy.102, f32[3,1,16,512]{3,2,1,0:T(8,128)S(1)} %collective-permute-done.4, f32[3,16,16,512]{3,2,1,0:T(8,128)S(1)} %broadcast_in_dim.9, f32[3,1,16,512]{3,2,1,0:T(8,128)S(1)} %collective-permute-done.5), kind=kLoop, calls=%fused_computation.23 | loop fusion | flops 5995296 | bytes 3989088 | tf_op jit(solution)/shard_map/concatenate | solution.py:23
  34.8 2.0 fusion.16
  36.9 1.3 collective-permute-start.8
  38.2 3.6 %collective-permute-start.9 = (f32[3,1,16,512]{3,2,1,0:T(8,128)S(1)}, f32[3,1,16,512]{3,2,1,0:T(8,128)S(1)}, u32[]{:S(2)}, u32[]{:S(2)}) collective-permute-start(f32[3,1,16,512]{3,2,1,0:T(8,128)S(1)} %get-tuple-element.105), channel_id=1, source_target_pairs={{0,16},{16,32},{32,48},{48,64},{64,80},{80,96},{96,112},{112,128},... | collective-permute-start | bytes 294920 | tf_op jit(solution)/shard_map/ppermute | solution.py:19
  42.9 2.9 collective-permute-start.10
  45.8 1.3 collective-permute-start.11
  47.1 1.3 collective-permute-done.10
  48.6 4.7 %collective-permute-done.11 = f32[3,18,1,512]{3,1,2,0:T(8,128)S(1)} collective-permute-done((f32[3,18,1,512]{3,1,2,0:T(8,128)S(1)}, f32[3,18,1,512]{3,1,2,0:T(8,128)S(1)}, u32[]{:S(2)}, u32[]{:S(2)}) %collective-permute-start.11) | collective-permute-done | bytes 110624 | tf_op jit(solution)/shard_map/ppermute | solution.py:19
  53.4 3.4 %select_maximum_fusion.8 = f32[3,18,18,514]{3,2,1,0:T(8,128)S(1)} fusion(f32[3,18,1,512]{3,2,1,0:T(1,128)S(1)} %copy.106, f32[3,18,1,512]{3,2,1,0:T(1,128)S(1)} %copy.108, f32[3,1,16,512]{3,2,1,0:T(8,128)S(1)} %collective-permute-done.8, f32[3,16,16,512]{3,2,1,0:T(8,128)S(1)} %fusion.16, f32[3,1,16,512]{3,2,1,0:T(8,128)S(1)} %collective-permute-done.9), kind=kLoop, calls=%fused_computation.19 | loop fusion | flops 5995296 | bytes 3989088 | tf_op jit(solution)/shard_map/concatenate | solution.py:23
  56.8 2.4 fusion.48
  59.3 1.3 collective-permute-start.12
  60.6 5.5 %collective-permute-start.13 = (f32[3,1,16,512]{3,2,1,0:T(8,128)S(1)}, f32[3,1,16,512]{3,2,1,0:T(8,128)S(1)}, u32[]{:S(2)}, u32[]{:S(2)}) collective-permute-start(f32[3,1,16,512]{3,2,1,0:T(8,128)S(1)} %get-tuple-element.103), channel_id=1, source_target_pairs={{0,16},{16,32},{32,48},{48,64},{64,80},{80,96},{96,112},{112,128},... | collective-permute-start | bytes 294920 | tf_op jit(solution)/shard_map/ppermute | solution.py:19
  67.3 5.1 %collective-permute-start.14 = (f32[3,18,1,512]{3,1,2,0:T(8,128)S(1)}, f32[3,18,1,512]{3,1,2,0:T(8,128)S(1)}, u32[]{:S(2)}, u32[]{:S(2)}) collective-permute-start(f32[3,18,1,512]{3,1,2,0:T(8,128)S(1)} %copy.111), channel_id=1, source_target_pairs={{1,0},{2,1},{3,2},{4,3},{5,4},{6,5},{7,6},{8,7},{9,8},{10,9},{11,1... | collective-permute-start | bytes 331784 | tf_op jit(solution)/shard_map/ppermute | solution.py:22
  72.4 1.5 collective-permute-start.15
  73.9 1.1 collective-permute-done.14
  75.2 4.3 %collective-permute-done.15 = f32[3,18,1,512]{3,1,2,0:T(8,128)S(1)} collective-permute-done((f32[3,18,1,512]{3,1,2,0:T(8,128)S(1)}, f32[3,18,1,512]{3,1,2,0:T(8,128)S(1)}, u32[]{:S(2)}, u32[]{:S(2)}) %collective-permute-start.15) | collective-permute-done | bytes 110624 | tf_op jit(solution)/shard_map/ppermute | solution.py:19
  79.6 3.4 %select_maximum_fusion.4 = f32[3,18,18,514]{3,2,1,0:T(8,128)S(1)} fusion(f32[3,18,1,512]{3,2,1,0:T(1,128)S(1)} %copy.112, f32[3,18,1,512]{3,2,1,0:T(1,128)S(1)} %copy.114, f32[3,1,16,512]{3,2,1,0:T(8,128)S(1)} %collective-permute-done.12, f32[3,16,16,512]{3,2,1,0:T(8,128)S(1)} %fusion.48, f32[3,1,16,512]{3,2,1,0:T(8,128)S(1)} %collective-permute-done.13), kind=kLoop, calls=%fused_computation.15 | loop fusion | flops 5995296 | bytes 3989088 | tf_op jit(solution)/shard_map/concatenate | solution.py:23
  83.1 2.4 fusion.34
  85.6 1.3 collective-permute-start.16
  86.9 5.6 %collective-permute-start.17 = (f32[3,1,16,512]{3,2,1,0:T(8,128)S(1)}, f32[3,1,16,512]{3,2,1,0:T(8,128)S(1)}, u32[]{:S(2)}, u32[]{:S(2)}) collective-permute-start(f32[3,1,16,512]{3,2,1,0:T(8,128)S(1)} %get-tuple-element.101), channel_id=1, source_target_pairs={{0,16},{16,32},{32,48},{48,64},{64,80},{80,96},{96,112},{112,128},... | collective-permute-start | bytes 294920 | tf_op jit(solution)/shard_map/ppermute | solution.py:19
  92.5 2.1 reshape_reshape.4
  95.5 4.3 %collective-permute-start.18 = (f32[3,18,1,512]{3,1,2,0:T(8,128)S(1)}, f32[3,18,1,512]{3,1,2,0:T(8,128)}, u32[]{:S(2)}, u32[]{:S(2)}) collective-permute-start(f32[3,18,1,512]{3,1,2,0:T(8,128)S(1)} %copy.117), channel_id=1, source_target_pairs={{1,0},{2,1},{3,2},{4,3},{5,4},{6,5},{7,6},{8,7},{9,8},{10,9},{11,1... | collective-permute-start | bytes 331784 | tf_op jit(solution)/shard_map/ppermute | solution.py:22
  100.5 1.3 collective-permute-start.19
  101.8 2.1 concatenate.171
  103.9 1.0 copy.118
  104.9 2.9 collective-permute-done.19
  107.8 1.0 copy.120
  108.9 3.4 %select_maximum_fusion = f32[3,18,18,514]{3,2,1,0:T(8,128)S(1)} fusion(f32[3,18,1,512]{3,2,1,0:T(1,128)S(1)} %copy.118, f32[3,18,1,512]{3,2,1,0:T(1,128)S(1)} %copy.120, f32[3,1,16,512]{3,2,1,0:T(8,128)S(1)} %collective-permute-done.16, f32[3,16,16,512]{3,2,1,0:T(8,128)S(1)} %fusion.34, f32[3,1,16,512]{3,2,1,0:T(8,128)S(1)} %collective-permute-done.17), kind=kLoop, calls=%fused_computation.11 | loop fusion | flops 5995296 | bytes 3989088 | tf_op jit(solution)/shard_map/concatenate | solution.py:23
  112.4 3.4 %fusion.20 = f32[3,16,16,512]{3,2,1,0:T(8,128)} fusion(f32[3,16,16,512]{3,2,1,0:T(8,128)S(1)} %copy-done.1, f32[3,18,18,514]{3,2,1,0:T(8,128)S(1)} %select_maximum_fusion, f32[3,18,1,512]{3,2,1,0:T(1,128)S(1)} %copy.120, f32[3,1,16,512]{3,2,1,0:T(8,128)S(1)} %collective-permute-done.16, f32[3,16,16,512]{3,2,1,0:T(8,128)S(1)} %fusion.34, ...), kind=kLoop, calls=%fused_computation.47 | loop fusion | flops 8650752 | bytes 11952128 | tf_op jit(solution)/shard_map/sub | solution.py:108
  115.8 2.0 concatenate.170
  117.9 1.5 maximum_bitcast_fusion
  119.4 134.5 %while.11 = (s32[]{:T(128)}, f32[4,512]{1,0:T(4,128)S(1)}, f32[8,8,4,2048]{3,1,0,2:T(8,128)}, s32[8,8,2048]{2,1,0:T(8,128)}, s32[]{:T(128)}, /*index=5*/s32[]{:T(128)}) while((s32[]{:T(128)}, f32[4,512]{1,0:T(4,128)S(1)}, f32[8,8,4,2048]{3,1,0,2:T(8,128)}, s32[8,8,2048]{2,1,0:T(8,128)}, s32[]{:T(128)}, /*index=5*/s32[]{:T(128)}) %tuple.60), condition=%wide.region_1.2_spmd.clone, body=%wide.region_0.1_spmd.clone.sunk | while | flops 411045888 | bytes 999511 | solution.py:85
  121.2 15.0 %fusion.84 = f32[4,512]{1,0:T(4,128)S(1)} fusion(s32[8,2048]{1,0:T(8,128)S(1)} %dynamic-slice_bitcast_fusion.2, f32[1,8,4,2048]{3,1,0,2:T(8,128)S(1)} %constant_dynamic-slice_fusion.2, f32[4,512]{1,0:T(4,128)S(1)} %get-tuple-element.157, pred[]{:T(512)S(6)} %compare.100), kind=kOutput, calls=%fused_computation.5.clone.1 | convolution fusion | flops 411045888 | bytes 344065 | tf_op jit(solution)/shard_map/while/body/eval_jaxpr/grk,gak->ra/dot_general | solution.py:81
  138.0 15.0 %fusion.84 = f32[4,512]{1,0:T(4,128)S(1)} fusion(s32[8,2048]{1,0:T(8,128)S(1)} %dynamic-slice_bitcast_fusion.2, f32[1,8,4,2048]{3,1,0,2:T(8,128)S(1)} %constant_dynamic-slice_fusion.2, f32[4,512]{1,0:T(4,128)S(1)} %get-tuple-element.157, pred[]{:T(512)S(6)} %compare.100), kind=kOutput, calls=%fused_computation.5.clone.1 | convolution fusion | flops 411045888 | bytes 344065 | tf_op jit(solution)/shard_map/while/body/eval_jaxpr/grk,gak->ra/dot_general | solution.py:81
  153.0 1.0 constant_dynamic-slice_fusion.2
  154.8 15.0 %fusion.84 = f32[4,512]{1,0:T(4,128)S(1)} fusion(s32[8,2048]{1,0:T(8,128)S(1)} %dynamic-slice_bitcast_fusion.2, f32[1,8,4,2048]{3,1,0,2:T(8,128)S(1)} %constant_dynamic-slice_fusion.2, f32[4,512]{1,0:T(4,128)S(1)} %get-tuple-element.157, pred[]{:T(512)S(6)} %compare.100), kind=kOutput, calls=%fused_computation.5.clone.1 | convolution fusion | flops 411045888 | bytes 344065 | tf_op jit(solution)/shard_map/while/body/eval_jaxpr/grk,gak->ra/dot_general | solution.py:81
  169.8 1.0 constant_dynamic-slice_fusion.2
  171.6 15.0 %fusion.84 = f32[4,512]{1,0:T(4,128)S(1)} fusion(s32[8,2048]{1,0:T(8,128)S(1)} %dynamic-slice_bitcast_fusion.2, f32[1,8,4,2048]{3,1,0,2:T(8,128)S(1)} %constant_dynamic-slice_fusion.2, f32[4,512]{1,0:T(4,128)S(1)} %get-tuple-element.157, pred[]{:T(512)S(6)} %compare.100), kind=kOutput, calls=%fused_computation.5.clone.1 | convolution fusion | flops 411045888 | bytes 344065 | tf_op jit(solution)/shard_map/while/body/eval_jaxpr/grk,gak->ra/dot_general | solution.py:81
  186.6 1.0 constant_dynamic-slice_fusion.2
  188.4 15.0 %fusion.84 = f32[4,512]{1,0:T(4,128)S(1)} fusion(s32[8,2048]{1,0:T(8,128)S(1)} %dynamic-slice_bitcast_fusion.2, f32[1,8,4,2048]{3,1,0,2:T(8,128)S(1)} %constant_dynamic-slice_fusion.2, f32[4,512]{1,0:T(4,128)S(1)} %get-tuple-element.157, pred[]{:T(512)S(6)} %compare.100), kind=kOutput, calls=%fused_computation.5.clone.1 | convolution fusion | flops 411045888 | bytes 344065 | tf_op jit(solution)/shard_map/while/body/eval_jaxpr/grk,gak->ra/dot_general | solution.py:81
  205.3 15.0 %fusion.84 = f32[4,512]{1,0:T(4,128)S(1)} fusion(s32[8,2048]{1,0:T(8,128)S(1)} %dynamic-slice_bitcast_fusion.2, f32[1,8,4,2048]{3,1,0,2:T(8,128)S(1)} %constant_dynamic-slice_fusion.2, f32[4,512]{1,0:T(4,128)S(1)} %get-tuple-element.157, pred[]{:T(512)S(6)} %compare.100), kind=kOutput, calls=%fused_computation.5.clone.1 | convolution fusion | flops 411045888 | bytes 344065 | tf_op jit(solution)/shard_map/while/body/eval_jaxpr/grk,gak->ra/dot_general | solution.py:81
  222.1 15.0 %fusion.84 = f32[4,512]{1,0:T(4,128)S(1)} fusion(s32[8,2048]{1,0:T(8,128)S(1)} %dynamic-slice_bitcast_fusion.2, f32[1,8,4,2048]{3,1,0,2:T(8,128)S(1)} %constant_dynamic-slice_fusion.2, f32[4,512]{1,0:T(4,128)S(1)} %get-tuple-element.157, pred[]{:T(512)S(6)} %compare.100), kind=kOutput, calls=%fused_computation.5.clone.1 | convolution fusion | flops 411045888 | bytes 344065 | tf_op jit(solution)/shard_map/while/body/eval_jaxpr/grk,gak->ra/dot_general | solution.py:81
  238.9 15.0 %fusion.84 = f32[4,512]{1,0:T(4,128)S(1)} fusion(s32[8,2048]{1,0:T(8,128)S(1)} %dynamic-slice_bitcast_fusion.2, f32[1,8,4,2048]{3,1,0,2:T(8,128)S(1)} %constant_dynamic-slice_fusion.2, f32[4,512]{1,0:T(4,128)S(1)} %get-tuple-element.157, pred[]{:T(512)S(6)} %compare.100), kind=kOutput, calls=%fused_computation.5.clone.1 | convolution fusion | flops 411045888 | bytes 344065 | tf_op jit(solution)/shard_map/while/body/eval_jaxpr/grk,gak->ra/dot_general | solution.py:81
  254.0 29.7 %all_to_all.5 = f32[32,4,512]{2,1,0:T(4,128)S(1)} all-to-all(f32[32,4,512]{2,1,0:T(4,128)S(1)} %broadcast_multiply_fusion.1), channel_id=1, replica_groups=mesh['gx'=32,'gy'=16] {'gx'}, dimensions={0} | all-to-all | bytes 524288 | tf_op jit(solution)/shard_map/all_to_all | solution.py:114
  283.8 2.2 collective-permute-start.21
  286.3 2.1 collective-permute-start.20
  288.5 2.5 collective-permute-start.23
  291.1 2.9 collective-permute-done.23
  294.0 3.1 collective-permute-start.25
  297.4 2.8 collective-permute-start.22
  301.0 2.0 collective-permute-done.22
  303.3 4.3 %collective-permute-start.24 = (f32[3,512]{1,0:T(4,128)S(1)}, f32[3,512]{1,0:T(4,128)S(1)}, u32[]{:S(2)}, u32[]{:S(2)}) collective-permute-start(f32[3,512]{1,0:T(4,128)S(1)} %subtract_subtract_fusion), channel_id=1, source_target_pairs={{0,64},{16,80},{32,96},{48,112},{64,0},{80,16},{96,32},{112,48},{1... | collective-permute-start | bytes 18440 | tf_op jit(solution)/shard_map/ppermute | solution.py:30
  307.6 2.7 collective-permute-done.24
  (128 shorter events, 22.1 us)
Async XLA Ops:
  1.4 3.0 collective-permute-start.1
  3.1 4.4 %collective-permute-start = (f32[1,16,512]{2,1,0:T(8,128)S(1)}, f32[1,16,512]{2,1,0:T(8,128)S(1)}, u32[]{:S(2)}, u32[]{:S(2)}) collective-permute-start(f32[1,16,512]{2,1,0:T(8,128)S(1)} %get-tuple-element.110), channel_id=1, source_target_pairs={{16,0},{32,16},{48,32},{64,48},{80,64},{96,80},{112,96},{128,112},... | collective-permute-start | bytes 98312 | tf_op jit(solution)/shard_map/ppermute | solution.py:22
  7.6 10.4 %collective-permute-start.2 = (f32[18,1,512]{2,1,0:T(1,128)S(1)}, f32[18,1,512]{2,1,0:T(1,128)S(1)}, u32[]{:S(2)}, u32[]{:S(2)}) collective-permute-start(f32[18,1,512]{2,1,0:T(1,128)S(1)} %get-tuple-element.108), channel_id=1, source_target_pairs={{1,0},{2,1},{3,2},{4,3},{5,4},{6,5},{7,6},{8,7},{9,8},{10,9},{11,1... | collective-permute-start | bytes 110600 | tf_op jit(solution)/shard_map/ppermute | solution.py:22
  10.5 7.5 %collective-permute-start.3 = (f32[18,1,512]{2,1,0:T(1,128)S(1)}, f32[18,1,512]{2,1,0:T(1,128)S(1)}, u32[]{:S(2)}, u32[]{:S(2)}) collective-permute-start(f32[18,1,512]{2,1,0:T(1,128)S(1)} %get-tuple-element.107), channel_id=1, source_target_pairs={{0,1},{1,2},{2,3},{3,4},{4,5},{5,6},{6,7},{7,8},{8,9},{9,10},{10,1... | collective-permute-start | bytes 110600 | tf_op jit(solution)/shard_map/ppermute | solution.py:19
  11.8 6.8 %collective-permute-start.4 = (f32[3,1,16,512]{3,2,1,0:T(8,128)S(1)}, f32[3,1,16,512]{3,2,1,0:T(8,128)S(1)}, u32[]{:S(2)}, u32[]{:S(2)}) collective-permute-start(f32[3,1,16,512]{3,2,1,0:T(8,128)S(1)} %broadcast.87), channel_id=1, source_target_pairs={{16,0},{32,16},{48,32},{64,48},{80,64},{96,80},{112,96},{128,112},... | collective-permute-start | bytes 294920 | tf_op jit(solution)/shard_map/ppermute | solution.py:22
  13.1 5.8 %collective-permute-start.5 = (f32[3,1,16,512]{3,2,1,0:T(8,128)S(1)}, f32[3,1,16,512]{3,2,1,0:T(8,128)S(1)}, u32[]{:S(2)}, u32[]{:S(2)}) collective-permute-start(f32[3,1,16,512]{3,2,1,0:T(8,128)S(1)} %broadcast.87), channel_id=1, source_target_pairs={{0,16},{16,32},{32,48},{48,64},{64,80},{80,96},{96,112},{112,128},... | collective-permute-start | bytes 294920 | tf_op jit(solution)/shard_map/ppermute | solution.py:19
  19.1 6.0 %copy-start.16 = (f32[16,16,512]{2,1,0:T(8,128)S(1)}, f32[16,16,512]{2,1,0:T(8,128)}, u32[]{:S(2)}) copy-start(f32[16,16,512]{2,1,0:T(8,128)} %param.8) | copy-start | bytes 1572868
  19.1 6.0 %copy-start.18 = (f32[16,16,512]{2,1,0:T(8,128)S(1)}, f32[16,16,512]{2,1,0:T(8,128)}, u32[]{:S(2)}) copy-start(f32[16,16,512]{2,1,0:T(8,128)} %param.9) | copy-start | bytes 1572868
  19.4 7.1 %collective-permute-start.6 = (f32[3,18,1,512]{3,1,2,0:T(8,128)S(1)}, f32[3,18,1,512]{3,1,2,0:T(8,128)S(1)}, u32[]{:S(2)}, u32[]{:S(2)}) collective-permute-start(f32[3,18,1,512]{3,1,2,0:T(8,128)S(1)} %copy.99), channel_id=1, source_target_pairs={{1,0},{2,1},{3,2},{4,3},{5,4},{6,5},{7,6},{8,7},{9,8},{10,9},{11,1... | collective-permute-start | bytes 331784 | tf_op jit(solution)/shard_map/ppermute | solution.py:22
  23.8 7.4 %collective-permute-start.7 = (f32[3,18,1,512]{3,1,2,0:T(8,128)S(1)}, f32[3,18,1,512]{3,1,2,0:T(8,128)S(1)}, u32[]{:S(2)}, u32[]{:S(2)}) collective-permute-start(f32[3,18,1,512]{3,1,2,0:T(8,128)S(1)} %copy.101), channel_id=1, source_target_pairs={{0,1},{1,2},{2,3},{3,4},{4,5},{5,6},{6,7},{7,8},{8,9},{9,10},{10,1... | collective-permute-start | bytes 331784 | tf_op jit(solution)/shard_map/ppermute | solution.py:19
  25.9 57.2 %copy-start.2 = (f32[16,16,512]{2,1,0:T(8,128)}, f32[16,16,512]{2,1,0:T(8,128)S(1)}, u32[]{:S(2)}) copy-start(f32[16,16,512]{2,1,0:T(8,128)S(1)} %get-tuple-element.86) | copy-start | bytes 1572868
  25.9 57.2 %copy-start.4 = (f32[16,16,512]{2,1,0:T(8,128)}, f32[16,16,512]{2,1,0:T(8,128)S(1)}, u32[]{:S(2)}) copy-start(f32[16,16,512]{2,1,0:T(8,128)S(1)} %get-tuple-element.87) | copy-start | bytes 1572868
  25.9 57.2 %copy-start.6 = (f32[16,16,512]{2,1,0:T(8,128)}, f32[16,16,512]{2,1,0:T(8,128)S(1)}, u32[]{:S(2)}) copy-start(f32[16,16,512]{2,1,0:T(8,128)S(1)} %get-tuple-element.88) | copy-start | bytes 1572868
  25.9 57.2 %copy-start.8 = (f32[16,16,512]{2,1,0:T(8,128)}, f32[16,16,512]{2,1,0:T(8,128)S(1)}, u32[]{:S(2)}) copy-start(f32[16,16,512]{2,1,0:T(8,128)S(1)} %get-tuple-element.89) | copy-start | bytes 1572868
  25.9 57.2 %copy-start.10 = (f32[16,16,512]{2,1,0:T(8,128)}, f32[16,16,512]{2,1,0:T(8,128)S(1)}, u32[]{:S(2)}) copy-start(f32[16,16,512]{2,1,0:T(8,128)S(1)} %get-tuple-element.90) | copy-start | bytes 1572868
  25.9 57.2 %copy-start.12 = (f32[16,16,512]{2,1,0:T(8,128)}, f32[16,16,512]{2,1,0:T(8,128)S(1)}, u32[]{:S(2)}) copy-start(f32[16,16,512]{2,1,0:T(8,128)S(1)} %get-tuple-element.91) | copy-start | bytes 1572868
  25.9 57.2 %copy-start.14 = (f32[16,16,512]{2,1,0:T(8,128)}, f32[16,16,512]{2,1,0:T(8,128)S(1)}, u32[]{:S(2)}) copy-start(f32[16,16,512]{2,1,0:T(8,128)S(1)} %get-tuple-element.92) | copy-start | bytes 1572868
  31.4 3.5 %copy-start.1 = (f32[3,16,16,512]{3,2,1,0:T(8,128)S(1)}, f32[3,16,16,512]{3,2,1,0:T(8,128)}, u32[]{:S(2)}) copy-start(f32[3,16,16,512]{3,2,1,0:T(8,128)} %param.7) | copy-start | bytes 4718596
  36.9 4.9 %collective-permute-start.8 = (f32[3,1,16,512]{3,2,1,0:T(8,128)S(1)}, f32[3,1,16,512]{3,2,1,0:T(8,128)S(1)}, u32[]{:S(2)}, u32[]{:S(2)}) collective-permute-start(f32[3,1,16,512]{3,2,1,0:T(8,128)S(1)} %get-tuple-element.106), channel_id=1, source_target_pairs={{16,0},{32,16},{48,32},{64,48},{80,64},{96,80},{112,96},{128,112},... | collective-permute-start | bytes 294920 | tf_op jit(solution)/shard_map/ppermute | solution.py:22
  38.2 4.5 %collective-permute-start.9 = (f32[3,1,16,512]{3,2,1,0:T(8,128)S(1)}, f32[3,1,16,512]{3,2,1,0:T(8,128)S(1)}, u32[]{:S(2)}, u32[]{:S(2)}) collective-permute-start(f32[3,1,16,512]{3,2,1,0:T(8,128)S(1)} %get-tuple-element.105), channel_id=1, source_target_pairs={{0,16},{16,32},{32,48},{48,64},{64,80},{80,96},{96,112},{112,128},... | collective-permute-start | bytes 294920 | tf_op jit(solution)/shard_map/ppermute | solution.py:19
  42.9 5.6 %collective-permute-start.10 = (f32[3,18,1,512]{3,1,2,0:T(8,128)S(1)}, f32[3,18,1,512]{3,1,2,0:T(8,128)S(1)}, u32[]{:S(2)}, u32[]{:S(2)}) collective-permute-start(f32[3,18,1,512]{3,1,2,0:T(8,128)S(1)} %copy.105), channel_id=1, source_target_pairs={{1,0},{2,1},{3,2},{4,3},{5,4},{6,5},{7,6},{8,7},{9,8},{10,9},{11,1... | collective-permute-start | bytes 331784 | tf_op jit(solution)/shard_map/ppermute | solution.py:22
  45.8 7.4 %collective-permute-start.11 = (f32[3,18,1,512]{3,1,2,0:T(8,128)S(1)}, f32[3,18,1,512]{3,1,2,0:T(8,128)S(1)}, u32[]{:S(2)}, u32[]{:S(2)}) collective-permute-start(f32[3,18,1,512]{3,1,2,0:T(8,128)S(1)} %copy.107), channel_id=1, source_target_pairs={{0,1},{1,2},{2,3},{3,4},{4,5},{5,6},{6,7},{7,8},{8,9},{9,10},{10,1... | collective-permute-start | bytes 331784 | tf_op jit(solution)/shard_map/ppermute | solution.py:19
  59.3 6.8 %collective-permute-start.12 = (f32[3,1,16,512]{3,2,1,0:T(8,128)S(1)}, f32[3,1,16,512]{3,2,1,0:T(8,128)S(1)}, u32[]{:S(2)}, u32[]{:S(2)}) collective-permute-start(f32[3,1,16,512]{3,2,1,0:T(8,128)S(1)} %get-tuple-element.104), channel_id=1, source_target_pairs={{16,0},{32,16},{48,32},{64,48},{80,64},{96,80},{112,96},{128,112},... | collective-permute-start | bytes 294920 | tf_op jit(solution)/shard_map/ppermute | solution.py:22
  60.6 6.4 %collective-permute-start.13 = (f32[3,1,16,512]{3,2,1,0:T(8,128)S(1)}, f32[3,1,16,512]{3,2,1,0:T(8,128)S(1)}, u32[]{:S(2)}, u32[]{:S(2)}) collective-permute-start(f32[3,1,16,512]{3,2,1,0:T(8,128)S(1)} %get-tuple-element.103), channel_id=1, source_target_pairs={{0,16},{16,32},{32,48},{48,64},{64,80},{80,96},{96,112},{112,128},... | collective-permute-start | bytes 294920 | tf_op jit(solution)/shard_map/ppermute | solution.py:19
  67.3 7.8 %collective-permute-start.14 = (f32[3,18,1,512]{3,1,2,0:T(8,128)S(1)}, f32[3,18,1,512]{3,1,2,0:T(8,128)S(1)}, u32[]{:S(2)}, u32[]{:S(2)}) collective-permute-start(f32[3,18,1,512]{3,1,2,0:T(8,128)S(1)} %copy.111), channel_id=1, source_target_pairs={{1,0},{2,1},{3,2},{4,3},{5,4},{6,5},{7,6},{8,7},{9,8},{10,9},{11,1... | collective-permute-start | bytes 331784 | tf_op jit(solution)/shard_map/ppermute | solution.py:22
  72.4 7.0 %collective-permute-start.15 = (f32[3,18,1,512]{3,1,2,0:T(8,128)S(1)}, f32[3,18,1,512]{3,1,2,0:T(8,128)S(1)}, u32[]{:S(2)}, u32[]{:S(2)}) collective-permute-start(f32[3,18,1,512]{3,1,2,0:T(8,128)S(1)} %copy.113), channel_id=1, source_target_pairs={{0,1},{1,2},{2,3},{3,4},{4,5},{5,6},{6,7},{7,8},{8,9},{9,10},{10,1... | collective-permute-start | bytes 331784 | tf_op jit(solution)/shard_map/ppermute | solution.py:19
  85.5 26.8 %copy-start = (f32[3,16,16,512]{3,2,1,0:T(8,128)}, f32[3,16,16,512]{3,2,1,0:T(8,128)S(1)}, u32[]{:S(2)}) copy-start(f32[3,16,16,512]{3,2,1,0:T(8,128)S(1)} %fusion.34) | copy-start | bytes 4718596
  85.6 9.7 %collective-permute-start.16 = (f32[3,1,16,512]{3,2,1,0:T(8,128)S(1)}, f32[3,1,16,512]{3,2,1,0:T(8,128)S(1)}, u32[]{:S(2)}, u32[]{:S(2)}) collective-permute-start(f32[3,1,16,512]{3,2,1,0:T(8,128)S(1)} %get-tuple-element.102), channel_id=1, source_target_pairs={{16,0},{32,16},{48,32},{64,48},{80,64},{96,80},{112,96},{128,112},... | collective-permute-start | bytes 294920 | tf_op jit(solution)/shard_map/ppermute | solution.py:22
  86.9 8.4 %collective-permute-start.17 = (f32[3,1,16,512]{3,2,1,0:T(8,128)S(1)}, f32[3,1,16,512]{3,2,1,0:T(8,128)S(1)}, u32[]{:S(2)}, u32[]{:S(2)}) collective-permute-start(f32[3,1,16,512]{3,2,1,0:T(8,128)S(1)} %get-tuple-element.101), channel_id=1, source_target_pairs={{0,16},{16,32},{32,48},{48,64},{64,80},{80,96},{96,112},{112,128},... | collective-permute-start | bytes 294920 | tf_op jit(solution)/shard_map/ppermute | solution.py:19
  95.5 8.4 %collective-permute-start.18 = (f32[3,18,1,512]{3,1,2,0:T(8,128)S(1)}, f32[3,18,1,512]{3,1,2,0:T(8,128)}, u32[]{:S(2)}, u32[]{:S(2)}) collective-permute-start(f32[3,18,1,512]{3,1,2,0:T(8,128)S(1)} %copy.117), channel_id=1, source_target_pairs={{1,0},{2,1},{3,2},{4,3},{5,4},{6,5},{7,6},{8,7},{9,8},{10,9},{11,1... | collective-permute-start | bytes 331784 | tf_op jit(solution)/shard_map/ppermute | solution.py:22
  100.5 7.3 %collective-permute-start.19 = (f32[3,18,1,512]{3,1,2,0:T(8,128)}, f32[3,18,1,512]{3,1,2,0:T(8,128)}, u32[]{:S(2)}, u32[]{:S(2)}) collective-permute-start(f32[3,18,1,512]{3,1,2,0:T(8,128)} %copy.119), channel_id=1, source_target_pairs={{0,1},{1,2},{2,3},{3,4},{4,5},{5,6},{6,7},{7,8},{8,9},{9,10},{10,1... | collective-permute-start | bytes 331784 | tf_op jit(solution)/shard_map/ppermute | solution.py:19
  108.8 3.5 %copy-start.3 = (f32[16,16,512]{2,1,0:T(8,128)S(1)}, f32[16,16,512]{2,1,0:T(8,128)}, u32[]{:S(2)}) copy-start(f32[16,16,512]{2,1,0:T(8,128)} %copy-done.2) | copy-start | bytes 1572868
  108.9 3.5 %copy-start.5 = (f32[16,16,512]{2,1,0:T(8,128)S(1)}, f32[16,16,512]{2,1,0:T(8,128)}, u32[]{:S(2)}) copy-start(f32[16,16,512]{2,1,0:T(8,128)} %copy-done.4) | copy-start | bytes 1572868
  108.9 3.5 %copy-start.7 = (f32[16,16,512]{2,1,0:T(8,128)S(1)}, f32[16,16,512]{2,1,0:T(8,128)}, u32[]{:S(2)}) copy-start(f32[16,16,512]{2,1,0:T(8,128)} %copy-done.6) | copy-start | bytes 1572868
  108.9 3.5 %copy-start.9 = (f32[16,16,512]{2,1,0:T(8,128)S(1)}, f32[16,16,512]{2,1,0:T(8,128)}, u32[]{:S(2)}) copy-start(f32[16,16,512]{2,1,0:T(8,128)} %copy-done.8) | copy-start | bytes 1572868
  108.9 3.5 %copy-start.11 = (f32[16,16,512]{2,1,0:T(8,128)S(1)}, f32[16,16,512]{2,1,0:T(8,128)}, u32[]{:S(2)}) copy-start(f32[16,16,512]{2,1,0:T(8,128)} %copy-done.10) | copy-start | bytes 1572868
  108.9 3.5 %copy-start.13 = (f32[16,16,512]{2,1,0:T(8,128)S(1)}, f32[16,16,512]{2,1,0:T(8,128)}, u32[]{:S(2)}) copy-start(f32[16,16,512]{2,1,0:T(8,128)} %copy-done.12) | copy-start | bytes 1572868
  108.9 3.5 %copy-start.15 = (f32[16,16,512]{2,1,0:T(8,128)S(1)}, f32[16,16,512]{2,1,0:T(8,128)}, u32[]{:S(2)}) copy-start(f32[16,16,512]{2,1,0:T(8,128)} %copy-done.14) | copy-start | bytes 1572868
  115.8 2.0 copy-start.17
  283.8 4.6 %collective-permute-start.21 = (f32[512]{0:T(512)S(1)}, f32[512]{0:T(512)S(1)}, u32[]{:S(2)}, u32[]{:S(2)}) collective-permute-start(f32[512]{0:T(512)S(1)} %bitcast.34), channel_id=1, source_target_pairs={{0,16},{16,0},{32,48},{48,32},{64,80},{80,64},{96,112},{112,96},{1... | collective-permute-start | bytes 6152 | tf_op jit(solution)/shard_map/ppermute | solution.py:30
  286.3 10.7 %collective-permute-start.20 = (f32[3,512]{1,0:T(4,128)S(1)}, f32[3,512]{1,0:T(4,128)S(1)}, u32[]{:S(2)}, u32[]{:S(2)}) collective-permute-start(f32[3,512]{1,0:T(4,128)S(1)} %subtract_subtract_fusion.2), channel_id=1, source_target_pairs={{0,16},{16,0},{32,48},{48,32},{64,80},{80,64},{96,112},{112,96},{1... | collective-permute-start | bytes 18440 | tf_op jit(solution)/shard_map/ppermute | solution.py:30
  288.5 5.5 %collective-permute-start.23 = (f32[512]{0:T(512)S(1)}, f32[512]{0:T(512)S(1)}, u32[]{:S(2)}, u32[]{:S(2)}) collective-permute-start(f32[512]{0:T(512)S(1)} %add.249), channel_id=1, source_target_pairs={{0,32},{16,48},{32,0},{48,16},{64,96},{80,112},{96,64},{112,80},{1... | collective-permute-start | bytes 6152 | tf_op jit(solution)/shard_map/ppermute | solution.py:30
  294.0 7.0 %collective-permute-start.25 = (f32[512]{0:T(512)S(1)}, f32[512]{0:T(512)S(1)}, u32[]{:S(2)}, u32[]{:S(2)}) collective-permute-start(f32[512]{0:T(512)S(1)} %add.254), channel_id=1, source_target_pairs={{0,64},{16,80},{32,96},{48,112},{64,0},{80,16},{96,32},{112,48},{1... | collective-permute-start | bytes 6152 | tf_op jit(solution)/shard_map/ppermute | solution.py:30
  297.4 5.5 %collective-permute-start.22 = (f32[3,512]{1,0:T(4,128)S(1)}, f32[3,512]{1,0:T(4,128)S(1)}, u32[]{:S(2)}, u32[]{:S(2)}) collective-permute-start(f32[3,512]{1,0:T(4,128)S(1)} %subtract_subtract_fusion.1), channel_id=1, source_target_pairs={{0,32},{16,48},{32,0},{48,16},{64,96},{80,112},{96,64},{112,80},{1... | collective-permute-start | bytes 18440 | tf_op jit(solution)/shard_map/ppermute | solution.py:30
  303.3 7.0 %collective-permute-start.24 = (f32[3,512]{1,0:T(4,128)S(1)}, f32[3,512]{1,0:T(4,128)S(1)}, u32[]{:S(2)}, u32[]{:S(2)}) collective-permute-start(f32[3,512]{1,0:T(4,128)S(1)} %subtract_subtract_fusion), channel_id=1, source_target_pairs={{0,64},{16,80},{32,96},{48,112},{64,0},{80,16},{96,32},{112,48},{1... | collective-permute-start | bytes 18440 | tf_op jit(solution)/shard_map/ppermute | solution.py:30
where the time goes:
time: 313 us; the launch traced here: 311 us
  matrix products  120 us (38%)
  starting transfers between devices  71 us (23%)
  waiting for transfers between devices  31.9 us (10%)
  blocking collectives  29.7 us (9%)
  other arithmetic  29.2 us (9%)
  local copies, waits for them, and re-layouts  27.2 us (9%)
    dot_general x8, matrix products, add_block(): jnp.einsum('grk,gak->ra', values, table, precision=lax.Precision.HIGHEST)  120 us
    all_to_all x1, blocking collectives, shards(): lax.all_to_all(outgoing, 'gx', split_axis=0, concat_axis=0, tiled=True)  29.7 us
    ppermute x10, starting transfers between devices, padded(): lax.ppermute(lax.slice_in_dim(block, block.shape[dim] - width, None, axis...  28 us
    ppermute x10, starting transfers between devices, padded(): lax.ppermute(lax.slice_in_dim(block, 0, width, axis=dim), axis, backward)  26.1 us
    ppermute x10, waiting for transfers between devices, padded(): lax.ppermute(lax.slice_in_dim(block, block.shape[dim] - width, None, axis...  18.7 us
    ppermute x6, starting transfers between devices, swapped(): return lax.ppermute(value, axis, pairs)  16.9 us
    concatenate x9, other arithmetic, padded(): block = jnp.concatenate([low, block, high], axis=dim)  15.1 us
    ppermute x6, waiting for transfers between devices, swapped(): return lax.ppermute(value, axis, pairs)  8.25 us
  transfers between devices with their start and end apart: 26, of which 15 were waited for; matrix products, arithmetic and copies ran while one was open for 3% of the time, Pallas kernels for 0%

commit v1 on v0

v1 whole, which is shorter than its diff:
```python
import jax
import jax.numpy as jnp
from jax import lax
from jax.experimental import pallas as pl
from jax.experimental.pallas import tpu as pltpu
from jax.sharding import PartitionSpec as P

COMP = 3
NAGG = 512
MERGES = 3
GROUP = 2**MERGES
LANES = 128
WIDE = 3
VWIDE = WIDE + 1
VISC_AT = COMP * WIDE
REACT_AT = VISC_AT + VWIDE
ROWS = REACT_AT + WIDE
X0 = 4
Y0 = 8
F32 = jnp.float32
BIG = 56 * 2**20


def pack_faces(rhs, visc, react, x_low, x_high, y_low, y_high):
    nx, ny, _ = visc.shape
    for c in range(COMP):
        for k in range(WIDE):
            x_low[c * WIDE + k] = rhs[c, k]
            x_high[c * WIDE + k] = rhs[c, nx - WIDE + k]
    for k in range(VWIDE):
        x_low[VISC_AT + k] = visc[k]
        x_high[VISC_AT + k] = visc[nx - VWIDE + k]
    for k in range(WIDE):
        x_low[REACT_AT + k] = react[k]
        x_high[REACT_AT + k] = react[nx - WIDE + k]
    for x in range(nx):
        for c in range(COMP):
            rows = pl.ds(c * WIDE, WIDE)
            y_low[x, rows] = rhs[c, x, pl.ds(0, WIDE)]
            y_high[x, rows] = rhs[c, x, pl.ds(ny - WIDE, WIDE)]
        rows = pl.ds(VISC_AT, VWIDE)
        y_low[x, rows] = visc[x, pl.ds(0, VWIDE)]
        y_high[x, rows] = visc[x, pl.ds(ny - VWIDE, VWIDE)]
        rows = pl.ds(REACT_AT, WIDE)
        y_low[x, rows] = react[x, pl.ds(0, WIDE)]
        y_high[x, rows] = react[x, pl.ds(ny - WIDE, WIDE)]


def corner_rows():
    table = []
    for away, at in ((1, 0), (2, 16), (3, 22)):
        left = WIDE - away
        if left:
            for c in range(COMP):
                table.append((away, "rhs", c, at, left))
                at += left
        table.append((away, "visc", 0, at, left + 1))
        at += left + 1
        if left:
            table.append((away, "react", 0, at, left))
    return table


def halo_index(side, away, kind, c):
    width = VWIDE if kind == "visc" else WIDE
    place = width - away if side == 0 else away - 1
    return {"rhs": c * WIDE, "visc": VISC_AT, "react": REACT_AT}[kind] + place


def pack_corners(from_low, from_high, y_low, y_high):
    ny = from_low.shape[1]
    for side, source in enumerate((from_low, from_high)):
        for away, kind, c, at, count in corner_rows():
            index = halo_index(side, away, kind, c)
            y_low[side, pl.ds(at, count)] = source[index, pl.ds(0, count)]
            y_high[side, pl.ds(at, count)] = source[index, pl.ds(ny - count, count)]


def chunks_of(value):
    return [value[..., c * LANES : (c + 1) * LANES] for c in range(value.shape[-1] // LANES)]


def z_up(parts):
    lane = lax.broadcasted_iota(jnp.int32, parts[0].shape, 1)
    turned = [pltpu.roll(p, LANES - 1, 1) for p in parts]
    turned.append(jnp.zeros_like(parts[0]))
    return [jnp.where(lane == LANES - 1, turned[i + 1], turned[i]) for i in range(len(parts))]


def z_down(parts):
    lane = lax.broadcasted_iota(jnp.int32, parts[0].shape, 1)
    turned = [jnp.zeros_like(parts[0])] + [pltpu.roll(p, 1, 1) for p in parts]
    return [jnp.where(lane == 0, turned[i], turned[i + 1]) for i in range(len(parts))]


def fine_kernel(
    rhs, visc, react, ids, x_low, x_high, y_low, y_high, c_low, c_high,
    vel_out, sums_out,
    visc_x, react_x, rhs_x, inv_x, wx, wy, wz, vel_a, vel_b, diag_s, terms,
):
    nx, ny, nz = visc.shape
    nc = nz // LANES

    def put(kind, c, x, rows, value):
        for i, part in enumerate(chunks_of(value)):
            if kind == "rhs":
                rhs_x[c, x, i, rows] = part
            elif kind == "visc":
                visc_x[x, i, rows] = part
            else:
                react_x[x, i, rows] = part

    own = pl.ds(Y0, ny)

    def fill(x, carry):
        for c in range(COMP):
            put("rhs", c, x + X0, own, rhs[c, x])
            at = pl.ds(c * WIDE, WIDE)
            put("rhs", c, x + X0, pl.ds(Y0 - WIDE, WIDE), y_low[x, at])
            put("rhs", c, x + X0, pl.ds(Y0 + ny, WIDE), y_high[x, at])
        put("visc", 0, x + X0, own, visc[x])
        at = pl.ds(VISC_AT, VWIDE)
        put("visc", 0, x + X0, pl.ds(Y0 - VWIDE, VWIDE), y_low[x, at])
        put("visc", 0, x + X0, pl.ds(Y0 + ny, VWIDE), y_high[x, at])
        put("react", 0, x + X0, own, react[x])
        at = pl.ds(REACT_AT, WIDE)
        put("react", 0, x + X0, pl.ds(Y0 - WIDE, WIDE), y_low[x, at])
        put("react", 0, x + X0, pl.ds(Y0 + ny, WIDE), y_high[x, at])
        return carry

    lax.fori_loop(0, nx, fill, 0)
    for side, source in enumerate((x_low, x_high)):
        for away in range(1, VWIDE + 1):
            x = X0 - away if side == 0 else X0 + nx - 1 + away
            put("visc", 0, x, own, source[halo_index(side, away, "visc", 0)])
            if away <= WIDE:
                for c in range(COMP):
                    put("rhs", c, x, own, source[halo_index(side, away, "rhs", c)])
                put("react", 0, x, own, source[halo_index(side, away, "react", 0)])
        for away, kind, c, at, count in corner_rows():
            x = X0 - away if side == 0 else X0 + nx - 1 + away
            put(kind, c, x, pl.ds(Y0 - count, count), c_low[side, pl.ds(at, count)])
            put(kind, c, x, pl.ds(Y0 + ny, count), c_high[side, pl.ds(at, count)])

    first, count = Y0 - WIDE, ny + 2 * WIDE
    mid = pl.ds(first, count)

    def prepare(x, carry):
        here = [visc_x[x, i, mid] for i in range(nc)]
        up = z_up(here)
        down = z_down(here)
        for i in range(nc):
            next_x = visc_x[x + 1, i, mid]
            next_y = visc_x[x, i, pl.ds(first + 1, count)]
            beside = next_x + visc_x[x - 1, i, mid]
            beside = beside + next_y + visc_x[x, i, pl.ds(first - 1, count)]
            beside = beside + up[i] + down[i]
            mass = react_x[x, i, mid]
            diag = mass + (3.0 * here[i] + 0.5 * beside)
            inv = jnp.where(mass > 0.0, 0.8 / diag, 0.0)
            diag_s[x, i, mid] = diag
            inv_x[x, i, mid] = inv
            wx[x, i, mid] = 0.5 * (here[i] + next_x)
            wy[x, i, mid] = 0.5 * (here[i] + next_y)
            wz[x, i, mid] = 0.5 * (here[i] + up[i])
            for c in range(COMP):
                vel_a[c, x, i, mid] = inv * rhs_x[c, x, i, mid]
        return carry

    lax.fori_loop(X0 - WIDE, X0 + nx + WIDE, prepare, 0)

    def besides(vel, c, x, first, count):
        rows = pl.ds(first, count)
        here = [vel[c, x, i, rows] for i in range(nc)]
        wz_here = [wz[x, i, rows] for i in range(nc)]
        up = z_up(here)
        down = z_down([wz_here[i] * here[i] for i in range(nc)])
        out = []
        for i in range(nc):
            total = wx[x, i, rows] * vel[c, x + 1, i, rows]
            total = total + wx[x - 1, i, rows] * vel[c, x - 1, i, rows]
            after, before = pl.ds(first + 1, count), pl.ds(first - 1, count)
            total = total + wy[x, i, rows] * vel[c, x, i, after]
            total = total + wy[x, i, before] * vel[c, x, i, before]
            out.append(total + wz_here[i] * up[i] + down[i])
        return here, out

    def sweep(source, target, reach):
        first, count = Y0 - reach, ny + 2 * reach
        rows = pl.ds(first, count)

        def step(x, carry):
            for c in range(COMP):
                here, beside = besides(source, c, x, first, count)
                for i in range(nc):
                    added = inv_x[x, i, rows] * (rhs_x[c, x, i, rows] + beside[i])
                    target[c, x, i, rows] = 0.2 * here[i] + added
            return carry

        lax.fori_loop(X0 - reach, X0 + nx + reach, step, 0)

    sweep(vel_a, vel_b, 2)
    sweep(vel_b, vel_a, 1)

    high = NAGG // LANES
    sub = lax.broadcasted_iota(jnp.int32, (2 * high, LANES), 0)
    in_high = sub % high
    is_first = sub < high
    label = lax.broadcasted_iota(jnp.int32, (LANES, LANES), 0)

    def gather(x, total):
        values = []
        for c in range(COMP):
            here, beside = besides(vel_a, c, x, Y0, ny)
            left = []
            for i in range(nc):
                vel_out[c, x - X0, :, i * LANES : (i + 1) * LANES] = here[i]
                left.append(rhs_x[c, x, i, own] - (diag_s[x, i, own] * here[i] - beside[i]))
            values.append(left)
        values.append([diag_s[x, i, own] for i in range(nc)])
        for t, value in enumerate(values):
            for i in range(nc):
                top = value[i].astype(jnp.bfloat16).astype(F32)
                terms[2 * t, i] = top
                terms[2 * t + 1, i] = value[i] - top
        for y in range(ny):
            left, right = [], []
            for i in range(nc):
                row = ids[x - X0, pl.ds(y, 1), i * LANES : (i + 1) * LANES]
                mask = (row >> 7) == in_high
                parts = []
                for t in range(COMP + 1):
                    top = terms[2 * t, i, pl.ds(y, 1)]
                    rest = terms[2 * t + 1, i, pl.ds(y, 1)]
                    parts.append(jnp.where(mask, jnp.where(is_first, top, rest), 0.0))
                left.append(jnp.concatenate(parts, axis=0).astype(jnp.bfloat16))
                hot = jnp.where((row & (LANES - 1)) == label, 1.0, 0.0)
                right.append(hot.astype(jnp.bfloat16))
            total = total + lax.dot_general(
                jnp.concatenate(left, axis=1),
                jnp.concatenate(right, axis=1),
                (((1,), (1,)), ((), ())),
                preferred_element_type=F32,
            )
        return total

    width = 2 * (COMP + 1) * high
    total = lax.fori_loop(X0, X0 + nx, gather, jnp.zeros((width, LANES), F32))
    for t in range(COMP + 1):
        at = 2 * high * t
        sums_out[pl.ds(high * t, high)] = total[at : at + high] + total[at + high : at + 2 * high]


def swapped(value, bit):
    row = lax.broadcasted_iota(jnp.int32, value.shape, 0)
    after = pltpu.roll(value, GROUP - bit, 0)
    before = pltpu.roll(value, bit, 0)
    return jnp.where((row & bit) == 0, after, before)


def coarse_kernel(place, arrived, out, levels):
    peers, rows, _ = arrived.shape
    flat = arrived.reshape(peers * rows, LANES)
    owner = flat[pl.ds(rows - 8, peers, stride=rows)]
    lane = lax.broadcasted_iota(jnp.int32, owner.shape, 1)
    base = place[0] - place[0] % GROUP
    chosen = jnp.where(owner == (base + lane).astype(F32), 1.0, 0.0)
    high = NAGG // LANES
    blocks = []
    for r in range((COMP + 1) * high):
        blocks.append(flat[pl.ds(r, peers, stride=rows)])
    gathered = jnp.concatenate(blocks, axis=1)
    owned = lax.dot_general(
        chosen, gathered, (((0,), (0,)), ((), ())),
        precision=lax.Precision.HIGHEST, preferred_element_type=F32,
    )[:GROUP]
    resid = [owned[:, c * NAGG : (c + 1) * NAGG] for c in range(COMP)]
    diag = 1.0 + owned[:, COMP * NAGG :]
    at = lax.broadcasted_iota(jnp.int32, diag.shape, 1)
    for level in range(MERGES + 1):
        coupling = 0.2 * jnp.minimum(diag, pltpu.roll(diag, NAGG - 1, 1))
        coupling = jnp.where(at == NAGG - 1, 0.0, coupling)

        def apply(vector):
            upper = coupling * pltpu.roll(vector, NAGG - 1, 1)
            lower = pltpu.roll(coupling * vector, 1, 1)
            return diag * vector - (upper + lower)

        left = []
        for c in range(COMP):
            correction = 0.8 * resid[c] / diag
            correction = correction + 0.8 * (resid[c] - apply(correction)) / diag
            levels[level, c] = correction
            out[level, pl.ds(c, 1)] = levels[level, c, pl.ds(place[0] % GROUP, 1)]
            if level < MERGES:
                rest = resid[c] - apply(correction)
                left.append(rest + swapped(rest, 2**level))
        if level < MERGES:
            resid = left
            diag = diag + swapped(diag, 2**level)


def shift(axis, value, by):
    count = lax.axis_size(axis)
    pairs = [(i, i + by) for i in range(count) if 0 <= i + by < count]
    return lax.ppermute(value, axis, pairs)


def shards(right_side, viscosity, reaction, agg_ids, owner_map):
    nx, ny, nz = viscosity.shape
    nc = nz // LANES
    x_message = jax.ShapeDtypeStruct((ROWS, ny, nz), F32)
    y_message = jax.ShapeDtypeStruct((nx, ROWS, nz), F32)
    to_x_low, to_x_high, to_y_low, to_y_high = pl.pallas_call(
        pack_faces,
        out_shape=(x_message, x_message, y_message, y_message),
        compiler_params=pltpu.CompilerParams(vmem_limit_bytes=BIG),
        name="pack_faces",
    )(right_side, viscosity, reaction)
    x_low = shift("gx", to_x_high, 1)
    x_high = shift("gx", to_x_low, -1)
    y_low = shift("gy", to_y_high, 1)
    y_high = shift("gy", to_y_low, -1)
    corner = jax.ShapeDtypeStruct((2, 24, nz), F32)
    to_c_low, to_c_high = pl.pallas_call(
        pack_corners,
        out_shape=(corner, corner),
        compiler_params=pltpu.CompilerParams(vmem_limit_bytes=BIG),
        name="pack_corners",
    )(x_low, x_high)
    c_low = shift("gy", to_c_high, 1)
    c_high = shift("gy", to_c_low, -1)

    wide = (nx + 2 * X0, nc, ny + 2 * Y0, LANES)
    high = NAGG // LANES
    velocity, sums = pl.pallas_call(
        fine_kernel,
        out_shape=(
            jax.ShapeDtypeStruct(right_side.shape, F32),
            jax.ShapeDtypeStruct(((COMP + 1) * high, LANES), F32),
        ),
        scratch_shapes=[
            pltpu.VMEM(wide, F32),
            pltpu.VMEM(wide, F32),
            pltpu.VMEM((COMP,) + wide, F32),
            pltpu.VMEM(wide, F32),
            pltpu.VMEM(wide, F32),
            pltpu.VMEM(wide, F32),
            pltpu.VMEM(wide, F32),
            pltpu.VMEM((COMP,) + wide, F32),
            pltpu.VMEM((COMP,) + wide, F32),
            pltpu.VMEM(wide, F32),
            pltpu.VMEM((2 * (COMP + 1), nc, ny, LANES), F32),
        ],
        compiler_params=pltpu.CompilerParams(vmem_limit_bytes=BIG),
        name="fine",
    )(right_side, viscosity, reaction, agg_ids, x_low, x_high, y_low, y_high, c_low, c_high)

    peers = lax.axis_size("gx")
    owner = jnp.broadcast_to(owner_map.astype(F32).reshape(1, 1), (8, LANES))
    packet = jnp.concatenate([sums, owner], axis=0)
    arrived = lax.all_to_all(
        jnp.broadcast_to(packet[None], (peers,) + packet.shape), "gx", 0, 0, tiled=True
    )
    place = lax.axis_index("gx").astype(jnp.int32).reshape(1)
    corrections = pl.pallas_call(
        coarse_kernel,
        out_shape=jax.ShapeDtypeStruct((MERGES + 1, COMP, NAGG), F32),
        in_specs=[
            pl.BlockSpec(memory_space=pltpu.SMEM),
            pl.BlockSpec(memory_space=pltpu.VMEM),
        ],
        scratch_shapes=[pltpu.VMEM((MERGES + 1, COMP, GROUP, NAGG), F32)],
        compiler_params=pltpu.CompilerParams(vmem_limit_bytes=BIG),
        name="coarse",
    )(place, arrived)
    return (velocity, corrections[None, None])


def solution(mesh):
    return jax.shard_map(
        shards,
        mesh=mesh,
        in_specs=(
            P(None, "gx", "gy", None),
            P("gx", "gy", None),
            P("gx", "gy", None),
            P("gx", "gy", None),
            P("gx", "gy"),
        ),
        out_specs=(P(None, "gx", "gy", None), P("gx", "gy", None, None, None)),
        check_vma=False,
    )
```

time: 313 us -> 85.3 us (0.27)
  the two profiles are of different devices: /device:TPU:480 before, /device:TPU:225 now
where the time goes in v1:
time: 85.3 us; the launch traced here: 84.8 us
  Pallas kernels  34.1 us (40%)
  starting transfers between devices  27.5 us (32%)
  waiting for transfers between devices  16.7 us (20%)
  local copies, waits for them, and re-layouts  5.06 us (6%)
  between operations  1.39 us (2%)
    pallas_call x1, Pallas kernels, shards(): pl.pallas_call(fine_kernel, out_shape=(jax.ShapeDtypeStruct(right_side.sh...  25.7 us
    ppermute x6, starting transfers between devices, shift(): return lax.ppermute(value, axis, pairs)  18.9 us
    all_to_all x1, waiting for transfers between devices, shards(): lax.all_to_all(jnp.broadcast_to(packet[None], (peers,) + packet.shape), '...  10.2 us
    all_to_all x1, starting transfers between devices, shards(): lax.all_to_all(jnp.broadcast_to(packet[None], (peers,) + packet.shape), '...  8.53 us
    ppermute x6, waiting for transfers between devices, shift(): return lax.ppermute(value, axis, pairs)  6.55 us
    unnamed x15, local copies, waits for them, and re-layouts  3.58 us
    pallas_call x1, Pallas kernels, shards(): pl.pallas_call(coarse_kernel, out_shape=jax.ShapeDtypeStruct((MERGES + 1,...  3.35 us
    pallas_call x1, Pallas kernels, shards(): pl.pallas_call(pack_faces, out_shape=(x_message, x_message, y_message, y_...  3.2 us
  transfers between devices with their start and end apart: 7, of which 4 were waited for; matrix products, arithmetic and copies ran while one was open for 0% of the time, Pallas kernels for 2%

profile of v1, /device:TPU:225, one launch (start us, length us, event | category | flops | bytes accessed | tf_op | source)
XLA Modules:
  0.0 84.8 jit_solution(12737044577097728352)
XLA Ops:
  0.6 3.2 %pack_faces.1 = (f32[16,16,512]{2,1,0:T(8,128)}, f32[16,16,512]{2,1,0:T(8,128)}, f32[16,16,512]{2,1,0:T(8,128)}, f32[16,16,512]{2,1,0:T(8,128)}) custom-call(f32[3,16,16,512]{3,2,1,0:T(8,128)} %rhs.3, f32[16,16,512]{2,1,0:T(8,128)} %visc.3, f32[16,16,512]{2,1,0:T(8,128)} %react.3), custom_call_target="tpu_custom_call" | custom-call | tf_op jit(solution)/shard_map/pack_faces/pallas_call | solution.py:314
  3.8 3.7 %collective-permute-start = (f32[16,16,512]{2,1,0:T(8,128)}, f32[16,16,512]{2,1,0:T(8,128)S(1)}, u32[]{:S(2)}, u32[]{:S(2)}) collective-permute-start(f32[16,16,512]{2,1,0:T(8,128)} %get-tuple-element.10), channel_id=1, source_target_pairs={{0,16},{16,32},{32,48},{48,64},{64,80},{80,96},{96,112},{112,128},... | collective-permute-start | bytes 1572872 | tf_op jit(solution)/shard_map/ppermute | solution.py:306
  7.5 1.9 %collective-permute-start.1 = (f32[16,16,512]{2,1,0:T(8,128)}, f32[16,16,512]{2,1,0:T(8,128)S(1)}, u32[]{:S(2)}, u32[]{:S(2)}) collective-permute-start(f32[16,16,512]{2,1,0:T(8,128)} %get-tuple-element.11), channel_id=1, source_target_pairs={{16,0},{32,16},{48,32},{64,48},{80,64},{96,80},{112,96},{128,112},... | collective-permute-start | bytes 1572872 | tf_op jit(solution)/shard_map/ppermute | solution.py:306
  9.4 4.8 %collective-permute-start.2 = (f32[16,16,512]{2,1,0:T(8,128)}, f32[16,16,512]{2,1,0:T(8,128)S(1)}, u32[]{:S(2)}, u32[]{:S(2)}) collective-permute-start(f32[16,16,512]{2,1,0:T(8,128)} %get-tuple-element.12), channel_id=1, source_target_pairs={{0,1},{1,2},{2,3},{3,4},{4,5},{5,6},{6,7},{7,8},{8,9},{9,10},{10,1... | collective-permute-start | bytes 1572872 | tf_op jit(solution)/shard_map/ppermute | solution.py:306
  14.2 1.9 %collective-permute-start.3 = (f32[16,16,512]{2,1,0:T(8,128)}, f32[16,16,512]{2,1,0:T(8,128)S(1)}, u32[]{:S(2)}, u32[]{:S(2)}) collective-permute-start(f32[16,16,512]{2,1,0:T(8,128)} %get-tuple-element.13), channel_id=1, source_target_pairs={{1,0},{2,1},{3,2},{4,3},{5,4},{6,5},{7,6},{8,7},{9,8},{10,9},{11,1... | collective-permute-start | bytes 1572872 | tf_op jit(solution)/shard_map/ppermute | solution.py:306
  16.1 0.0 collective-permute-done.from_low.x_low
  16.1 0.0 copy-start
  16.1 2.4 %collective-permute-done.1.from_high.x_high = f32[16,16,512]{2,1,0:T(8,128)S(1)} collective-permute-done((f32[16,16,512]{2,1,0:T(8,128)}, f32[16,16,512]{2,1,0:T(8,128)S(1)}, u32[]{:S(2)}, u32[]{:S(2)}) %collective-permute-start.1) | collective-permute-done | bytes 524320 | tf_op jit(solution)/shard_map/ppermute | solution.py:306
  18.5 0.0 copy-done
  18.5 0.0 copy-start.1
  18.5 0.8 copy-done.1
  19.3 1.9 %pack_corners.1 = (f32[2,24,512]{2,1,0:T(8,128)}, f32[2,24,512]{2,1,0:T(8,128)}) custom-call(f32[16,16,512]{2,1,0:T(8,128)} %copy-done, f32[16,16,512]{2,1,0:T(8,128)} %copy-done.1), custom_call_target="tpu_custom_call" | custom-call | tf_op jit(solution)/shard_map/pack_corners/pallas_call | solution.py:325
  21.2 4.7 %collective-permute-start.4 = (f32[2,24,512]{2,1,0:T(8,128)}, f32[2,24,512]{2,1,0:T(8,128)S(1)}, u32[]{:S(2)}, u32[]{:S(2)}) collective-permute-start(f32[2,24,512]{2,1,0:T(8,128)} %get-tuple-element.14), channel_id=1, source_target_pairs={{0,1},{1,2},{2,3},{3,4},{4,5},{5,6},{6,7},{7,8},{8,9},{9,10},{10,1... | collective-permute-start | bytes 294920 | tf_op jit(solution)/shard_map/ppermute | solution.py:306
  26.0 1.9 %collective-permute-start.5 = (f32[2,24,512]{2,1,0:T(8,128)}, f32[2,24,512]{2,1,0:T(8,128)S(1)}, u32[]{:S(2)}, u32[]{:S(2)}) collective-permute-start(f32[2,24,512]{2,1,0:T(8,128)} %get-tuple-element.15), channel_id=1, source_target_pairs={{1,0},{2,1},{3,2},{4,3},{5,4},{6,5},{7,6},{8,7},{9,8},{10,9},{11,1... | collective-permute-start | bytes 294920 | tf_op jit(solution)/shard_map/ppermute | solution.py:306
  28.6 0.0 collective-permute-done.2.y_low
  28.6 0.0 copy-start.3
  28.6 2.3 %collective-permute-done.3.y_high = f32[16,16,512]{2,1,0:T(8,128)S(1)} collective-permute-done((f32[16,16,512]{2,1,0:T(8,128)}, f32[16,16,512]{2,1,0:T(8,128)S(1)}, u32[]{:S(2)}, u32[]{:S(2)}) %collective-permute-start.3) | collective-permute-done | bytes 524320 | tf_op jit(solution)/shard_map/ppermute | solution.py:306
  30.9 0.0 copy-start.4
  30.9 0.0 collective-permute-done.4.c_low
  30.9 0.0 copy-start.5
  30.9 1.8 %collective-permute-done.5.c_high = f32[2,24,512]{2,1,0:T(8,128)S(1)} collective-permute-done((f32[2,24,512]{2,1,0:T(8,128)}, f32[2,24,512]{2,1,0:T(8,128)S(1)}, u32[]{:S(2)}, u32[]{:S(2)}) %collective-permute-start.5) | collective-permute-done | bytes 98336 | tf_op jit(solution)/shard_map/ppermute | solution.py:306
  32.8 0.0 copy-done.3
  32.8 0.0 copy-done.4
  32.8 0.0 copy-done.5
  32.8 0.0 copy-start.6
  32.8 0.6 copy-done.6
  33.4 25.7 %fine.1 = (f32[3,16,16,512]{3,2,1,0:T(8,128)}, f32[16,128]{1,0:T(8,128)}) custom-call(f32[3,16,16,512]{3,2,1,0:T(8,128)} %rhs.3, f32[16,16,512]{2,1,0:T(8,128)} %visc.3, f32[16,16,512]{2,1,0:T(8,128)} %react.3, s32[16,16,512]{2,1,0:T(8,128)} %ids.1, f32[16,16,512]{2,1,0:T(8,128)} %copy-done, f32[16,16,512]{2,1,0:T(8,128)} %copy-done.1, ...), custom_call_target="tpu_custom_call" | custom-call | tf_op jit(solution)/shard_map/fine/pallas_call | solution.py:336
  59.1 0.7 concatenate.3
  59.8 0.8 broadcast_in_dim.7
  60.6 8.5 %all-to-all-start = ((f32[32,24,128]{2,1,0:T(8,128)}), f32[32,24,128]{2,1,0:T(8,128)S(1)}, u32[]{:S(2)}, u32[]{:S(2)}) async-start(f32[32,24,128]{2,1,0:T(8,128)} %broadcast_in_dim.7), calls=%async_computation | async-start | bytes 786432 | tf_op jit(solution)/shard_map/all_to_all | solution.py:362
  69.1 10.2 %all-to-all-done.arrived = f32[32,24,128]{2,1,0:T(8,128)S(1)} async-done(((f32[32,24,128]{2,1,0:T(8,128)}), f32[32,24,128]{2,1,0:T(8,128)S(1)}, u32[]{:S(2)}, u32[]{:S(2)}) %all-to-all-start) | async-done | bytes 393248 | tf_op jit(solution)/shard_map/all_to_all | solution.py:362
  79.3 0.0 copy-start.2
  79.3 0.8 copy-done.2
  80.0 3.3 %coarse.1 = f32[4,3,512]{2,1,0:T(4,128)} custom-call(s32[1]{0:T(128)} %bitcast.place, f32[32,24,128]{2,1,0:T(8,128)} %copy-done.2), custom_call_target="tpu_custom_call" | custom-call | tf_op jit(solution)/shard_map/coarse/pallas_call | solution.py:366
  83.4 1.4 %copy.7 = f32[1,1,4,3,512]{4,2,3,1,0:T(4,128)} copy(f32[1,1,4,3,512]{4,3,2,1,0:T(4,128)} %bitcast.3) | data formatting | bytes 49152
Async XLA Ops:
  3.8 12.3 %collective-permute-start = (f32[16,16,512]{2,1,0:T(8,128)}, f32[16,16,512]{2,1,0:T(8,128)S(1)}, u32[]{:S(2)}, u32[]{:S(2)}) collective-permute-start(f32[16,16,512]{2,1,0:T(8,128)} %get-tuple-element.10), channel_id=1, source_target_pairs={{0,16},{16,32},{32,48},{48,64},{64,80},{80,96},{96,112},{112,128},... | collective-permute-start | bytes 1572872 | tf_op jit(solution)/shard_map/ppermute | solution.py:306
  7.5 11.0 %collective-permute-start.1 = (f32[16,16,512]{2,1,0:T(8,128)}, f32[16,16,512]{2,1,0:T(8,128)S(1)}, u32[]{:S(2)}, u32[]{:S(2)}) collective-permute-start(f32[16,16,512]{2,1,0:T(8,128)} %get-tuple-element.11), channel_id=1, source_target_pairs={{16,0},{32,16},{48,32},{64,48},{80,64},{96,80},{112,96},{128,112},... | collective-permute-start | bytes 1572872 | tf_op jit(solution)/shard_map/ppermute | solution.py:306
  9.4 19.1 %collective-permute-start.2 = (f32[16,16,512]{2,1,0:T(8,128)}, f32[16,16,512]{2,1,0:T(8,128)S(1)}, u32[]{:S(2)}, u32[]{:S(2)}) collective-permute-start(f32[16,16,512]{2,1,0:T(8,128)} %get-tuple-element.12), channel_id=1, source_target_pairs={{0,1},{1,2},{2,3},{3,4},{4,5},{5,6},{6,7},{7,8},{8,9},{9,10},{10,1... | collective-permute-start | bytes 1572872 | tf_op jit(solution)/shard_map/ppermute | solution.py:306
  14.2 16.7 %collective-permute-start.3 = (f32[16,16,512]{2,1,0:T(8,128)}, f32[16,16,512]{2,1,0:T(8,128)S(1)}, u32[]{:S(2)}, u32[]{:S(2)}) collective-permute-start(f32[16,16,512]{2,1,0:T(8,128)} %get-tuple-element.13), channel_id=1, source_target_pairs={{1,0},{2,1},{3,2},{4,3},{5,4},{6,5},{7,6},{8,7},{9,8},{10,9},{11,1... | collective-permute-start | bytes 1572872 | tf_op jit(solution)/shard_map/ppermute | solution.py:306
  16.1 2.4 %copy-start = (f32[16,16,512]{2,1,0:T(8,128)}, f32[16,16,512]{2,1,0:T(8,128)S(1)}, u32[]{:S(2)}) copy-start(f32[16,16,512]{2,1,0:T(8,128)S(1)} %collective-permute-done.from_low.x_low) | copy-start | bytes 1572868
  18.5 0.8 copy-start.1
  21.2 9.7 %collective-permute-start.4 = (f32[2,24,512]{2,1,0:T(8,128)}, f32[2,24,512]{2,1,0:T(8,128)S(1)}, u32[]{:S(2)}, u32[]{:S(2)}) collective-permute-start(f32[2,24,512]{2,1,0:T(8,128)} %get-tuple-element.14), channel_id=1, source_target_pairs={{0,1},{1,2},{2,3},{3,4},{4,5},{5,6},{6,7},{7,8},{8,9},{9,10},{10,1... | collective-permute-start | bytes 294920 | tf_op jit(solution)/shard_map/ppermute | solution.py:306
  26.0 6.8 %collective-permute-start.5 = (f32[2,24,512]{2,1,0:T(8,128)}, f32[2,24,512]{2,1,0:T(8,128)S(1)}, u32[]{:S(2)}, u32[]{:S(2)}) collective-permute-start(f32[2,24,512]{2,1,0:T(8,128)} %get-tuple-element.15), channel_id=1, source_target_pairs={{1,0},{2,1},{3,2},{4,3},{5,4},{6,5},{7,6},{8,7},{9,8},{10,9},{11,1... | collective-permute-start | bytes 294920 | tf_op jit(solution)/shard_map/ppermute | solution.py:306
  28.6 4.2 %copy-start.3 = (f32[16,16,512]{2,1,0:T(8,128)}, f32[16,16,512]{2,1,0:T(8,128)S(1)}, u32[]{:S(2)}) copy-start(f32[16,16,512]{2,1,0:T(8,128)S(1)} %collective-permute-done.2.y_low) | copy-start | bytes 1572868
  30.9 1.9 %copy-start.4 = (f32[16,16,512]{2,1,0:T(8,128)}, f32[16,16,512]{2,1,0:T(8,128)S(1)}, u32[]{:S(2)}) copy-start(f32[16,16,512]{2,1,0:T(8,128)S(1)} %collective-permute-done.3.y_high) | copy-start | bytes 1572868
  30.9 1.9 %copy-start.5 = (f32[2,24,512]{2,1,0:T(8,128)}, f32[2,24,512]{2,1,0:T(8,128)S(1)}, u32[]{:S(2)}) copy-start(f32[2,24,512]{2,1,0:T(8,128)S(1)} %collective-permute-done.4.c_low) | copy-start | bytes 294916
  32.8 0.6 copy-start.6
  60.6 18.7 %all-to-all-start = ((f32[32,24,128]{2,1,0:T(8,128)}), f32[32,24,128]{2,1,0:T(8,128)S(1)}, u32[]{:S(2)}, u32[]{:S(2)}) async-start(f32[32,24,128]{2,1,0:T(8,128)} %broadcast_in_dim.7), calls=%async_computation | async-start | bytes 786432 | tf_op jit(solution)/shard_map/all_to_all | solution.py:362
  79.3 0.8 copy-start.2

commit v2 on v1

--- a/solution.py
+++ b/solution.py
@@ -18,7 +18,11 @@
 X0 = 4
 Y0 = 8
 F32 = jnp.float32
-BIG = 56 * 2**20
+HIGH = 8
+LOW = NAGG // HIGH
+SUM_ROWS = (COMP + 1) * NAGG // LANES
+BIG = 36 * 2**20
+SMALL = 8 * 2**20
 
 
 def pack_faces(rhs, visc, react, x_low, x_high, y_low, y_high):
@@ -94,9 +98,9 @@
 
 
 def fine_kernel(
-    rhs, visc, react, ids, x_low, x_high, y_low, y_high, c_low, c_high,
-    vel_out, sums_out,
-    visc_x, react_x, rhs_x, inv_x, wx, wy, wz, vel_a, vel_b, diag_s, terms,
+    owner, rhs, visc, react, ids, x_low, x_high, y_low, y_high, c_low, c_high,
+    vel_out, packets,
+    visc_x, react_x, rhs_x, inv_x, wx, wy, wz, vel_a, vel_b, diag_s, terms, low_s, high_s, sums,
 ):
     nx, ny, nz = visc.shape
     nc = nz // LANES
@@ -202,11 +206,10 @@
     sweep(vel_a, vel_b, 2)
     sweep(vel_b, vel_a, 1)
 
-    high = NAGG // LANES
-    sub = lax.broadcasted_iota(jnp.int32, (2 * high, LANES), 0)
-    in_high = sub % high
-    is_first = sub < high
-    label = lax.broadcasted_iota(jnp.int32, (LANES, LANES), 0)
+    in_high = lax.broadcasted_iota(jnp.int32, (HIGH, LANES), 0)
+    label = lax.broadcasted_iota(jnp.int32, (LOW, LANES), 0).astype(F32)
+    label = label.astype(jnp.bfloat16).reshape(LOW // 16, 16, LANES)
+    ones, zeros = jnp.ones_like(label), jnp.zeros_like(label)
 
     def gather(x, total):
         values = []
@@ -223,19 +226,20 @@
                 top = value[i].astype(jnp.bfloat16).astype(F32)
                 terms[2 * t, i] = top
                 terms[2 * t + 1, i] = value[i] - top
+        for i in range(nc):
+            ident = ids[x - X0, :, i * LANES : (i + 1) * LANES]
+            low_s[i] = (ident % LOW).astype(F32)
+            high_s[i] = ident // LOW
         for y in range(ny):
             left, right = [], []
+            row = pl.ds(y, 1)
             for i in range(nc):
-                row = ids[x - X0, pl.ds(y, 1), i * LANES : (i + 1) * LANES]
-                mask = (row >> 7) == in_high
-                parts = []
-                for t in range(COMP + 1):
-                    top = terms[2 * t, i, pl.ds(y, 1)]
-                    rest = terms[2 * t + 1, i, pl.ds(y, 1)]
-                    parts.append(jnp.where(mask, jnp.where(is_first, top, rest), 0.0))
+                mask = high_s[i, row] == in_high
+                parts = [jnp.where(mask, terms[t, i, row], 0.0) for t in range(2 * (COMP + 1))]
                 left.append(jnp.concatenate(parts, axis=0).astype(jnp.bfloat16))
-                hot = jnp.where((row & (LANES - 1)) == label, 1.0, 0.0)
-                right.append(hot.astype(jnp.bfloat16))
+                low = jnp.broadcast_to(low_s[i, row], (16, LANES)).astype(jnp.bfloat16)
+                hot = jnp.where(low[None] == label, ones, zeros)
+                right.append(hot.reshape(LOW, LANES))
             total = total + lax.dot_general(
                 jnp.concatenate(left, axis=1),
                 jnp.concatenate(right, axis=1),
@@ -244,11 +248,21 @@
             )
         return total
 
-    width = 2 * (COMP + 1) * high
-    total = lax.fori_loop(X0, X0 + nx, gather, jnp.zeros((width, LANES), F32))
+    width = 2 * (COMP + 1) * HIGH
+    total = lax.fori_loop(X0, X0 + nx, gather, jnp.zeros((width, LOW), F32))
     for t in range(COMP + 1):
-        at = 2 * high * t
-        sums_out[pl.ds(high * t, high)] = total[at : at + high] + total[at + high : at + 2 * high]
+        at = 2 * HIGH * t
+        both = total[at : at + HIGH] + total[at + HIGH : at + 2 * HIGH]
+        sums[pl.ds(HIGH * t, HIGH), pl.ds(0, LOW)] = both
+    half = SUM_ROWS
+    even = sums[pl.ds(0, half, stride=2)]
+    odd = sums[pl.ds(1, half, stride=2)]
+    lane = lax.broadcasted_iota(jnp.int32, even.shape, 1)
+    packet = jnp.where(lane < LOW, even, pltpu.roll(odd, LOW, 1))
+    mine = jnp.full((8, LANES), owner[0, 0], jnp.int32).astype(F32)
+    for peer in range(packets.shape[0]):
+        packets[peer, pl.ds(0, SUM_ROWS)] = packet
+        packets[peer, pl.ds(SUM_ROWS, 8)] = mine
 
 
 def swapped(value, bit):
@@ -265,9 +279,8 @@
     lane = lax.broadcasted_iota(jnp.int32, owner.shape, 1)
     base = place[0] - place[0] % GROUP
     chosen = jnp.where(owner == (base + lane).astype(F32), 1.0, 0.0)
-    high = NAGG // LANES
     blocks = []
-    for r in range((COMP + 1) * high):
+    for r in range(SUM_ROWS):
         blocks.append(flat[pl.ds(r, peers, stride=rows)])
     gathered = jnp.concatenate(blocks, axis=1)
     owned = lax.dot_general(
@@ -291,7 +304,7 @@
             correction = 0.8 * resid[c] / diag
             correction = correction + 0.8 * (resid[c] - apply(correction)) / diag
             levels[level, c] = correction
-            out[level, pl.ds(c, 1)] = levels[level, c, pl.ds(place[0] % GROUP, 1)]
+            out[c, pl.ds(level, 1)] = levels[level, c, pl.ds(place[0] % GROUP, 1)]
             if level < MERGES:
                 rest = resid[c] - apply(correction)
                 left.append(rest + swapped(rest, 2**level))
@@ -314,7 +327,7 @@
     to_x_low, to_x_high, to_y_low, to_y_high = pl.pallas_call(
         pack_faces,
         out_shape=(x_message, x_message, y_message, y_message),
-        compiler_params=pltpu.CompilerParams(vmem_limit_bytes=BIG),
+        compiler_params=pltpu.CompilerParams(vmem_limit_bytes=SMALL),
         name="pack_faces",
     )(right_side, viscosity, reaction)
     x_low = shift("gx", to_x_high, 1)
@@ -325,20 +338,22 @@
     to_c_low, to_c_high = pl.pallas_call(
         pack_corners,
         out_shape=(corner, corner),
-        compiler_params=pltpu.CompilerParams(vmem_limit_bytes=BIG),
+        compiler_params=pltpu.CompilerParams(vmem_limit_bytes=SMALL),
         name="pack_corners",
     )(x_low, x_high)
     c_low = shift("gy", to_c_high, 1)
     c_high = shift("gy", to_c_low, -1)
 
     wide = (nx + 2 * X0, nc, ny + 2 * Y0, LANES)
-    high = NAGG // LANES
-    velocity, sums = pl.pallas_call(
+    peers = lax.axis_size("gx")
+    velocity, packets = pl.pallas_call(
         fine_kernel,
         out_shape=(
             jax.ShapeDtypeStruct(right_side.shape, F32),
-            jax.ShapeDtypeStruct(((COMP + 1) * high, LANES), F32),
+            jax.ShapeDtypeStruct((peers, SUM_ROWS + 8, LANES), F32),
         ),
+        in_specs=[pl.BlockSpec(memory_space=pltpu.SMEM)]
+        + [pl.BlockSpec(memory_space=pltpu.VMEM)] * 10,
         scratch_shapes=[
             pltpu.VMEM(wide, F32),
             pltpu.VMEM(wide, F32),
@@ -351,30 +366,27 @@
             pltpu.VMEM((COMP,) + wide, F32),
             pltpu.VMEM(wide, F32),
             pltpu.VMEM((2 * (COMP + 1), nc, ny, LANES), F32),
+            pltpu.VMEM((nc, ny, LANES), F32),
+            pltpu.VMEM((nc, ny, LANES), jnp.int32),
+            pltpu.VMEM((2 * SUM_ROWS, LANES), F32),
         ],
         compiler_params=pltpu.CompilerParams(vmem_limit_bytes=BIG),
         name="fine",
-    )(right_side, viscosity, reaction, agg_ids, x_low, x_high, y_low, y_high, c_low, c_high)
-
-    peers = lax.axis_size("gx")
-    owner = jnp.broadcast_to(owner_map.astype(F32).reshape(1, 1), (8, LANES))
-    packet = jnp.concatenate([sums, owner], axis=0)
-    arrived = lax.all_to_all(
-        jnp.broadcast_to(packet[None], (peers,) + packet.shape), "gx", 0, 0, tiled=True
-    )
+    )(owner_map, right_side, viscosity, reaction, agg_ids, x_low, x_high, y_low, y_high, c_low, c_high)
+    arrived = lax.all_to_all(packets, "gx", 0, 0, tiled=True)
     place = lax.axis_index("gx").astype(jnp.int32).reshape(1)
     corrections = pl.pallas_call(
         coarse_kernel,
-        out_shape=jax.ShapeDtypeStruct((MERGES + 1, COMP, NAGG), F32),
+        out_shape=jax.ShapeDtypeStruct((COMP, MERGES + 1, NAGG), F32),
         in_specs=[
             pl.BlockSpec(memory_space=pltpu.SMEM),
             pl.BlockSpec(memory_space=pltpu.VMEM),
         ],
         scratch_shapes=[pltpu.VMEM((MERGES + 1, COMP, GROUP, NAGG), F32)],
-        compiler_params=pltpu.CompilerParams(vmem_limit_bytes=BIG),
+        compiler_params=pltpu.CompilerParams(vmem_limit_bytes=SMALL),
         name="coarse",
     )(place, arrived)
-    return (velocity, corrections[None, None])
+    return (velocity, corrections.transpose(1, 0, 2)[None, None])
 
 
 def solution(mesh):

time: 85.3 us -> 72.5 us (0.85)
  Pallas kernels: 34.1 us -> 21 us
  waiting for transfers between devices: 16.7 us -> 18.6 us
  local copies, waits for them, and re-layouts: 5.06 us -> 3.5 us
    pallas_call x1, Pallas kernels: 25.7 us -> 18.2 us  [shards(): pl.pallas_call(fine_kernel, out_shape=(jax.ShapeDtypeStruct(right_side.sh...]
    pallas_call x1, Pallas kernels: 3.2 us -> 0.36 us  [shards(): pl.pallas_call(pack_faces, out_shape=(x_message, x_message, y_message, y_...]
    pallas_call x1, Pallas kernels: 1.92 us -> 0.06 us  [shards(): pl.pallas_call(pack_corners, out_shape=(corner, corner), compiler_params=...]
    ppermute x6, waiting for transfers between devices: 6.55 us -> 8.39 us  [shift(): return lax.ppermute(value, axis, pairs)]
    pallas_call x1, Pallas kernels: 3.35 us -> 2.35 us  [shards(): pl.pallas_call(coarse_kernel, out_shape=jax.ShapeDtypeStruct((COMP, MERGE...]
    unnamed x15 -> x14, local copies, waits for them, and re-layouts: 3.58 us -> 3.5 us
  transfers between devices with their start and end apart: 7 -> 7, of which waited for: 4 -> 4; matrix products, arithmetic and copies ran while one was open for 0% -> 0% of each run, Pallas kernels for 2% -> 0%
where the time goes in v2:
time: 72.5 us; the launch traced here: 72.1 us
  starting transfers between devices  27.7 us (38%)
  Pallas kernels  21 us (29%)
  waiting for transfers between devices  18.6 us (26%)
  local copies, waits for them, and re-layouts  3.5 us (5%)
  between operations  1.39 us (2%)
    ppermute x6, starting transfers between devices, shift(): return lax.ppermute(value, axis, pairs)  19.1 us
    pallas_call x1, Pallas kernels, shards(): pl.pallas_call(fine_kernel, out_shape=(jax.ShapeDtypeStruct(right_side.sh...  18.2 us
    all_to_all x1, waiting for transfers between devices, shards(): arrived = lax.all_to_all(packets, 'gx', 0, 0, tiled=True)  10.2 us
    all_to_all x1, starting transfers between devices, shards(): arrived = lax.all_to_all(packets, 'gx', 0, 0, tiled=True)  8.6 us
    ppermute x6, waiting for transfers between devices, shift(): return lax.ppermute(value, axis, pairs)  8.39 us
    unnamed x14, local copies, waits for them, and re-layouts  3.5 us
    pallas_call x1, Pallas kernels, shards(): pl.pallas_call(coarse_kernel, out_shape=jax.ShapeDtypeStruct((COMP, MERGE...  2.35 us
  transfers between devices with their start and end apart: 7, of which 4 were waited for; matrix products, arithmetic and copies ran while one was open for 0% of the time, Pallas kernels for 0%

profile of v2, /device:TPU:225, one launch (start us, length us, event | category | flops | bytes accessed | tf_op | source)
XLA Modules:
  0.0 72.1 jit_solution(4295916287296242051)
XLA Ops:
  0.6 0.0 copy-start
  0.6 1.4 %copy-done = f32[3,16,16,512]{3,2,1,0:T(8,128)S(1)} copy-done((f32[3,16,16,512]{3,2,1,0:T(8,128)S(1)}, f32[3,16,16,512]{3,2,1,0:T(8,128)}, u32[]{:S(2)}) %copy-start) | copy-done | bytes 1572888
  2.0 0.0 copy-start.2
  2.0 1.0 %copy-done.2 = f32[16,16,512]{2,1,0:T(8,128)S(1)} copy-done((f32[16,16,512]{2,1,0:T(8,128)S(1)}, f32[16,16,512]{2,1,0:T(8,128)}, u32[]{:S(2)}) %copy-start.2) | copy-done | bytes 524312
  3.1 0.0 copy-start.4
  3.1 1.0 %copy-done.4 = f32[16,16,512]{2,1,0:T(8,128)S(1)} copy-done((f32[16,16,512]{2,1,0:T(8,128)S(1)}, f32[16,16,512]{2,1,0:T(8,128)}, u32[]{:S(2)}) %copy-start.4) | copy-done | bytes 524312
  4.1 0.0 copy-start.1
  4.1 0.0 copy-start.3
  4.1 0.0 copy-start.5
  4.1 0.0 copy-start.6
  4.1 0.4 pack_faces.1
  4.5 3.8 %collective-permute-start = (f32[16,16,512]{2,1,0:T(8,128)S(1)}, f32[16,16,512]{2,1,0:T(8,128)S(1)}, u32[]{:S(2)}, u32[]{:S(2)}) collective-permute-start(f32[16,16,512]{2,1,0:T(8,128)S(1)} %get-tuple-element.10), channel_id=1, source_target_pairs={{0,16},{16,32},{32,48},{48,64},{64,80},{80,96},{96,112},{112,128},... | collective-permute-start | bytes 1572872 | tf_op jit(solution)/shard_map/ppermute | solution.py:319
  8.3 1.9 %collective-permute-start.1 = (f32[16,16,512]{2,1,0:T(8,128)S(1)}, f32[16,16,512]{2,1,0:T(8,128)S(1)}, u32[]{:S(2)}, u32[]{:S(2)}) collective-permute-start(f32[16,16,512]{2,1,0:T(8,128)S(1)} %get-tuple-element.11), channel_id=1, source_target_pairs={{16,0},{32,16},{48,32},{64,48},{80,64},{96,80},{112,96},{128,112},... | collective-permute-start | bytes 1572872 | tf_op jit(solution)/shard_map/ppermute | solution.py:319
  10.2 4.8 %collective-permute-start.2 = (f32[16,16,512]{2,1,0:T(8,128)S(1)}, f32[16,16,512]{2,1,0:T(8,128)S(1)}, u32[]{:S(2)}, u32[]{:S(2)}) collective-permute-start(f32[16,16,512]{2,1,0:T(8,128)S(1)} %get-tuple-element.12), channel_id=1, source_target_pairs={{0,1},{1,2},{2,3},{3,4},{4,5},{5,6},{6,7},{7,8},{8,9},{9,10},{10,1... | collective-permute-start | bytes 1572872 | tf_op jit(solution)/shard_map/ppermute | solution.py:319
  15.0 1.9 %collective-permute-start.3 = (f32[16,16,512]{2,1,0:T(8,128)S(1)}, f32[16,16,512]{2,1,0:T(8,128)S(1)}, u32[]{:S(2)}, u32[]{:S(2)}) collective-permute-start(f32[16,16,512]{2,1,0:T(8,128)S(1)} %get-tuple-element.13), channel_id=1, source_target_pairs={{1,0},{2,1},{3,2},{4,3},{5,4},{6,5},{7,6},{8,7},{9,8},{10,9},{11,1... | collective-permute-start | bytes 1572872 | tf_op jit(solution)/shard_map/ppermute | solution.py:319
  16.9 0.0 collective-permute-done.from_low.x_low
  17.0 2.2 %collective-permute-done.1.from_high.x_high = f32[16,16,512]{2,1,0:T(8,128)S(1)} collective-permute-done((f32[16,16,512]{2,1,0:T(8,128)S(1)}, f32[16,16,512]{2,1,0:T(8,128)S(1)}, u32[]{:S(2)}, u32[]{:S(2)}) %collective-permute-start.1) | collective-permute-done | bytes 524320 | tf_op jit(solution)/shard_map/ppermute | solution.py:319
  19.1 0.1 pack_corners.1
  19.2 4.8 %collective-permute-start.4 = (f32[2,24,512]{2,1,0:T(8,128)S(1)}, f32[2,24,512]{2,1,0:T(8,128)S(1)}, u32[]{:S(2)}, u32[]{:S(2)}) collective-permute-start(f32[2,24,512]{2,1,0:T(8,128)S(1)} %get-tuple-element.14), channel_id=1, source_target_pairs={{0,1},{1,2},{2,3},{3,4},{4,5},{5,6},{6,7},{7,8},{8,9},{9,10},{10,1... | collective-permute-start | bytes 294920 | tf_op jit(solution)/shard_map/ppermute | solution.py:319
  23.9 1.9 %collective-permute-start.5 = (f32[2,24,512]{2,1,0:T(8,128)S(1)}, f32[2,24,512]{2,1,0:T(8,128)S(1)}, u32[]{:S(2)}, u32[]{:S(2)}) collective-permute-start(f32[2,24,512]{2,1,0:T(8,128)S(1)} %get-tuple-element.15), channel_id=1, source_target_pairs={{1,0},{2,1},{3,2},{4,3},{5,4},{6,5},{7,6},{8,7},{9,8},{10,9},{11,1... | collective-permute-start | bytes 294920 | tf_op jit(solution)/shard_map/ppermute | solution.py:319
  26.5 0.0 collective-permute-done.2.y_low
  26.5 5.4 %collective-permute-done.3.y_high = f32[16,16,512]{2,1,0:T(8,128)S(1)} collective-permute-done((f32[16,16,512]{2,1,0:T(8,128)S(1)}, f32[16,16,512]{2,1,0:T(8,128)S(1)}, u32[]{:S(2)}, u32[]{:S(2)}) %collective-permute-start.3) | collective-permute-done | bytes 524320 | tf_op jit(solution)/shard_map/ppermute | solution.py:319
  31.9 0.0 collective-permute-done.4.c_low
  31.9 0.8 %collective-permute-done.5.c_high = f32[2,24,512]{2,1,0:T(8,128)S(1)} collective-permute-done((f32[2,24,512]{2,1,0:T(8,128)S(1)}, f32[2,24,512]{2,1,0:T(8,128)S(1)}, u32[]{:S(2)}, u32[]{:S(2)}) %collective-permute-start.5) | collective-permute-done | bytes 98336 | tf_op jit(solution)/shard_map/ppermute | solution.py:319
  32.8 0.0 copy-done.1
  32.8 0.0 copy-done.3
  32.8 0.0 copy-done.5
  32.8 0.0 copy-done.6
  32.8 18.2 %fine.1 = (f32[3,16,16,512]{3,2,1,0:T(8,128)}, f32[32,24,128]{2,1,0:T(8,128)}) custom-call(s32[1,1]{1,0:T(1,128)S(6)} %copy.7.owner, f32[3,16,16,512]{3,2,1,0:T(8,128)S(1)} %copy-done.1, f32[16,16,512]{2,1,0:T(8,128)S(1)} %copy-done.3, f32[16,16,512]{2,1,0:T(8,128)S(1)} %copy-done.5, s32[16,16,512]{2,1,0:T(8,128)S(1)} %copy-done.6, ...), custom_call_target="tpu_custom_call" | custom-call | tf_op jit(solution)/shard_map/fine/pallas_call | solution.py:349
  51.0 8.6 %all-to-all-start = ((f32[32,24,128]{2,1,0:T(8,128)}), f32[32,24,128]{2,1,0:T(8,128)S(1)}, u32[]{:S(2)}, u32[]{:S(2)}) async-start(f32[32,24,128]{2,1,0:T(8,128)} %get-tuple-element.17), calls=%async_computation | async-start | bytes 786432 | tf_op jit(solution)/shard_map/all_to_all | solution.py:376
  59.6 10.2 %all-to-all-done.arrived = f32[32,24,128]{2,1,0:T(8,128)S(1)} async-done(((f32[32,24,128]{2,1,0:T(8,128)}), f32[32,24,128]{2,1,0:T(8,128)S(1)}, u32[]{:S(2)}, u32[]{:S(2)}) %all-to-all-start) | async-done | bytes 393248 | tf_op jit(solution)/shard_map/all_to_all | solution.py:376
  69.7 2.4 %coarse.1 = f32[3,4,512]{2,1,0:T(4,128)} custom-call(s32[1]{0:T(128)} %bitcast.place, f32[32,24,128]{2,1,0:T(8,128)S(1)} %all-to-all-done.arrived), custom_call_target="tpu_custom_call" | custom-call | tf_op jit(solution)/shard_map/coarse/pallas_call | solution.py:378
Async XLA Ops:
  0.6 1.4 %copy-start = (f32[3,16,16,512]{3,2,1,0:T(8,128)S(1)}, f32[3,16,16,512]{3,2,1,0:T(8,128)}, u32[]{:S(2)}) copy-start(f32[3,16,16,512]{3,2,1,0:T(8,128)} %rhs.3) | copy-start | bytes 4718596
  2.0 1.0 %copy-start.2 = (f32[16,16,512]{2,1,0:T(8,128)S(1)}, f32[16,16,512]{2,1,0:T(8,128)}, u32[]{:S(2)}) copy-start(f32[16,16,512]{2,1,0:T(8,128)} %visc.3) | copy-start | bytes 1572868
  3.1 1.0 %copy-start.4 = (f32[16,16,512]{2,1,0:T(8,128)S(1)}, f32[16,16,512]{2,1,0:T(8,128)}, u32[]{:S(2)}) copy-start(f32[16,16,512]{2,1,0:T(8,128)} %react.3) | copy-start | bytes 1572868
  4.1 28.6 %copy-start.1 = (f32[3,16,16,512]{3,2,1,0:T(8,128)S(1)}, f32[3,16,16,512]{3,2,1,0:T(8,128)}, u32[]{:S(2)}) copy-start(f32[3,16,16,512]{3,2,1,0:T(8,128)} %rhs.3) | copy-start | bytes 4718596
  4.1 28.6 %copy-start.3 = (f32[16,16,512]{2,1,0:T(8,128)S(1)}, f32[16,16,512]{2,1,0:T(8,128)}, u32[]{:S(2)}) copy-start(f32[16,16,512]{2,1,0:T(8,128)} %visc.3) | copy-start | bytes 1572868
  4.1 28.6 %copy-start.5 = (f32[16,16,512]{2,1,0:T(8,128)S(1)}, f32[16,16,512]{2,1,0:T(8,128)}, u32[]{:S(2)}) copy-start(f32[16,16,512]{2,1,0:T(8,128)} %react.3) | copy-start | bytes 1572868
  4.1 28.6 %copy-start.6 = (s32[16,16,512]{2,1,0:T(8,128)S(1)}, s32[16,16,512]{2,1,0:T(8,128)}, u32[]{:S(2)}) copy-start(s32[16,16,512]{2,1,0:T(8,128)} %ids.1) | copy-start | bytes 1572868
  4.5 12.4 %collective-permute-start = (f32[16,16,512]{2,1,0:T(8,128)S(1)}, f32[16,16,512]{2,1,0:T(8,128)S(1)}, u32[]{:S(2)}, u32[]{:S(2)}) collective-permute-start(f32[16,16,512]{2,1,0:T(8,128)S(1)} %get-tuple-element.10), channel_id=1, source_target_pairs={{0,16},{16,32},{32,48},{48,64},{64,80},{80,96},{96,112},{112,128},... | collective-permute-start | bytes 1572872 | tf_op jit(solution)/shard_map/ppermute | solution.py:319
  8.3 10.8 %collective-permute-start.1 = (f32[16,16,512]{2,1,0:T(8,128)S(1)}, f32[16,16,512]{2,1,0:T(8,128)S(1)}, u32[]{:S(2)}, u32[]{:S(2)}) collective-permute-start(f32[16,16,512]{2,1,0:T(8,128)S(1)} %get-tuple-element.11), channel_id=1, source_target_pairs={{16,0},{32,16},{48,32},{64,48},{80,64},{96,80},{112,96},{128,112},... | collective-permute-start | bytes 1572872 | tf_op jit(solution)/shard_map/ppermute | solution.py:319
  10.2 16.3 %collective-permute-start.2 = (f32[16,16,512]{2,1,0:T(8,128)S(1)}, f32[16,16,512]{2,1,0:T(8,128)S(1)}, u32[]{:S(2)}, u32[]{:S(2)}) collective-permute-start(f32[16,16,512]{2,1,0:T(8,128)S(1)} %get-tuple-element.12), channel_id=1, source_target_pairs={{0,1},{1,2},{2,3},{3,4},{4,5},{5,6},{6,7},{7,8},{8,9},{9,10},{10,1... | collective-permute-start | bytes 1572872 | tf_op jit(solution)/shard_map/ppermute | solution.py:319
  15.0 16.9 %collective-permute-start.3 = (f32[16,16,512]{2,1,0:T(8,128)S(1)}, f32[16,16,512]{2,1,0:T(8,128)S(1)}, u32[]{:S(2)}, u32[]{:S(2)}) collective-permute-start(f32[16,16,512]{2,1,0:T(8,128)S(1)} %get-tuple-element.13), channel_id=1, source_target_pairs={{1,0},{2,1},{3,2},{4,3},{5,4},{6,5},{7,6},{8,7},{9,8},{10,9},{11,1... | collective-permute-start | bytes 1572872 | tf_op jit(solution)/shard_map/ppermute | solution.py:319
  19.2 12.7 %collective-permute-start.4 = (f32[2,24,512]{2,1,0:T(8,128)S(1)}, f32[2,24,512]{2,1,0:T(8,128)S(1)}, u32[]{:S(2)}, u32[]{:S(2)}) collective-permute-start(f32[2,24,512]{2,1,0:T(8,128)S(1)} %get-tuple-element.14), channel_id=1, source_target_pairs={{0,1},{1,2},{2,3},{3,4},{4,5},{5,6},{6,7},{7,8},{8,9},{9,10},{10,1... | collective-permute-start | bytes 294920 | tf_op jit(solution)/shard_map/ppermute | solution.py:319
  23.9 8.8 %collective-permute-start.5 = (f32[2,24,512]{2,1,0:T(8,128)S(1)}, f32[2,24,512]{2,1,0:T(8,128)S(1)}, u32[]{:S(2)}, u32[]{:S(2)}) collective-permute-start(f32[2,24,512]{2,1,0:T(8,128)S(1)} %get-tuple-element.15), channel_id=1, source_target_pairs={{1,0},{2,1},{3,2},{4,3},{5,4},{6,5},{7,6},{8,7},{9,8},{10,9},{11,1... | collective-permute-start | bytes 294920 | tf_op jit(solution)/shard_map/ppermute | solution.py:319
  51.0 18.8 %all-to-all-start = ((f32[32,24,128]{2,1,0:T(8,128)}), f32[32,24,128]{2,1,0:T(8,128)S(1)}, u32[]{:S(2)}, u32[]{:S(2)}) async-start(f32[32,24,128]{2,1,0:T(8,128)} %get-tuple-element.17), calls=%async_computation | async-start | bytes 786432 | tf_op jit(solution)/shard_map/all_to_all | solution.py:376

commit v3 on v2

v3 whole, which is shorter than its diff:
```python
import jax
import jax.numpy as jnp
from jax import lax
from jax.experimental import pallas as pl
from jax.experimental.pallas import tpu as pltpu
from jax.sharding import PartitionSpec as P

COMP = 3
NAGG = 512
MERGES = 3
GROUP = 2**MERGES
LANES = 128
WIDE = 3
VWIDE = WIDE + 1
VISC_AT = COMP * WIDE
REACT_AT = VISC_AT + VWIDE
ROWS = REACT_AT + WIDE
X0 = VWIDE
Y0 = VWIDE
F32 = jnp.float32
HIGH = 8
LOW = NAGG // HIGH
SUM_ROWS = (COMP + 1) * NAGG // LANES
BIG = 32 * 2**20
SMALL = 8 * 2**20


def corner_rows():
    table = []
    for away, at in ((1, 0), (2, 16), (3, 22)):
        left = WIDE - away
        if left:
            for c in range(COMP):
                table.append((away, "rhs", c, at, left))
                at += left
        table.append((away, "visc", 0, at, left + 1))
        at += left + 1
        if left:
            table.append((away, "react", 0, at, left))
    return table


def pack_y(rhs, visc, react, y_low, y_high):
    nx, ny, _ = visc.shape
    for x in range(nx):
        for c in range(COMP):
            rows = pl.ds(c * WIDE, WIDE)
            y_low[x, rows] = rhs[c, x, pl.ds(0, WIDE)]
            y_high[x, rows] = rhs[c, x, pl.ds(ny - WIDE, WIDE)]
        rows = pl.ds(VISC_AT, VWIDE)
        y_low[x, rows] = visc[x, pl.ds(0, VWIDE)]
        y_high[x, rows] = visc[x, pl.ds(ny - VWIDE, VWIDE)]
        rows = pl.ds(REACT_AT, WIDE)
        y_low[x, rows] = react[x, pl.ds(0, WIDE)]
        y_high[x, rows] = react[x, pl.ds(ny - WIDE, WIDE)]


def pack_corners(place, near, far, c_low, c_high):
    ny = near.shape[1]
    even = place[0] % 2 == 0
    for side, (source, at_high) in enumerate(((near, even), (far, jnp.logical_not(even)))):
        for away, kind, c, at, count in corner_rows():
            width = VWIDE if kind == "visc" else WIDE
            first = {"rhs": c * WIDE, "visc": VISC_AT, "react": REACT_AT}[kind]
            index = first + jnp.where(at_high, away - 1, width - away)
            rows = pl.ds(at, count)
            c_low[side, rows] = source[index, pl.ds(0, count)]
            c_high[side, rows] = source[index, pl.ds(ny - count, count)]


def chunks_of(value):
    return [value[..., c * LANES : (c + 1) * LANES] for c in range(value.shape[-1] // LANES)]


def z_up(parts):
    lane = lax.broadcasted_iota(jnp.int32, parts[0].shape, 1)
    turned = [pltpu.roll(p, LANES - 1, 1) for p in parts]
    turned.append(jnp.zeros_like(parts[0]))
    return [jnp.where(lane == LANES - 1, turned[i + 1], turned[i]) for i in range(len(parts))]


def z_down(parts):
    lane = lax.broadcasted_iota(jnp.int32, parts[0].shape, 1)
    turned = [jnp.zeros_like(parts[0])] + [pltpu.roll(p, 1, 1) for p in parts]
    return [jnp.where(lane == 0, turned[i], turned[i + 1]) for i in range(len(parts))]


def fine_kernel(
    place, owner, rhs, visc, react, ids, near, far, y_low, y_high, c_low, c_high,
    vel_out, packets,
    half_x, react_x, rhs_x, inv_x, vel_a, vel_b, diag_s, terms, low_s, high_s, sums,
):
    nx, ny, nz = visc.shape
    nc = nz // LANES

    def put(kind, c, x, rows, value):
        for i, part in enumerate(chunks_of(value)):
            if kind == "rhs":
                rhs_x[c, x, i, rows] = part
            elif kind == "visc":
                half_x[x, i, rows] = 0.5 * part
            else:
                react_x[x, i, rows] = part

    own = pl.ds(Y0, ny)

    def fill(x, carry):
        for c in range(COMP):
            put("rhs", c, x + X0, own, rhs[c, x])
            at = pl.ds(c * WIDE, WIDE)
            put("rhs", c, x + X0, pl.ds(Y0 - WIDE, WIDE), y_low[x, at])
            put("rhs", c, x + X0, pl.ds(Y0 + ny, WIDE), y_high[x, at])
        put("visc", 0, x + X0, own, visc[x])
        at = pl.ds(VISC_AT, VWIDE)
        put("visc", 0, x + X0, pl.ds(Y0 - VWIDE, VWIDE), y_low[x, at])
        put("visc", 0, x + X0, pl.ds(Y0 + ny, VWIDE), y_high[x, at])
        put("react", 0, x + X0, own, react[x])
        at = pl.ds(REACT_AT, WIDE)
        put("react", 0, x + X0, pl.ds(Y0 - WIDE, WIDE), y_low[x, at])
        put("react", 0, x + X0, pl.ds(Y0 + ny, WIDE), y_high[x, at])
        return carry

    lax.fori_loop(0, nx, fill, 0)
    even = place[0] % 2 == 0
    for source, at_high in ((near, even), (far, jnp.logical_not(even))):
        for away in range(1, VWIDE + 1):
            x = jnp.where(at_high, X0 + nx - 1 + away, X0 - away)
            place_v = jnp.where(at_high, away - 1, VWIDE - away)
            put("visc", 0, x, own, source[VISC_AT + place_v])
            if away <= WIDE:
                place_w = jnp.where(at_high, away - 1, WIDE - away)
                for c in range(COMP):
                    put("rhs", c, x, own, source[c * WIDE + place_w])
                put("react", 0, x, own, source[REACT_AT + place_w])
    for side, at_high in enumerate((even, jnp.logical_not(even))):
        for away, kind, c, at, count in corner_rows():
            before, after = pl.ds(Y0 - count, count), pl.ds(Y0 + ny, count)
            x = jnp.where(at_high, X0 + nx - 1 + away, X0 - away)
            put(kind, c, x, before, c_low[side, pl.ds(at, count)])
            put(kind, c, x, after, c_high[side, pl.ds(at, count)])

    def y_up(value):
        return pltpu.roll(value, value.shape[0] - 1, 0)

    def y_down(value):
        return pltpu.roll(value, 1, 0)

    def prepare(x, carry):
        here = [half_x[x, i] for i in range(nc)]
        up = z_up(here)
        down = z_down(here)
        for i in range(nc):
            beside = half_x[x + 1, i] + half_x[x - 1, i]
            beside = beside + y_up(here[i]) + y_down(here[i])
            beside = beside + up[i] + down[i]
            mass = react_x[x, i]
            diag = mass + (6.0 * here[i] + beside)
            inv = jnp.where(mass > 0.0, 0.8 / diag, 0.0)
            diag_s[x, i] = diag
            inv_x[x, i] = inv
            for c in range(COMP):
                vel_a[c, x, i] = inv * rhs_x[c, x, i]
        return carry

    lax.fori_loop(X0 - WIDE, X0 + nx + WIDE, prepare, 0, unroll=11)

    def stencil(vel, x, emit):
        shape = half_x.shape[2:]
        lane = lax.broadcasted_iota(jnp.int32, shape, 1)
        is_first, is_last = lane == 0, lane == LANES - 1
        none = jnp.zeros(shape, F32)
        half = [half_x[x, i] for i in range(nc)]
        half_up = [pltpu.roll(h, LANES - 1, 1) for h in half] + [none]
        here = [[vel[c, x, i] for i in range(nc)] for c in range(COMP)]
        turned = [[pltpu.roll(h, LANES - 1, 1) for h in part] + [none] for part in here]
        last = [none] * COMP
        for i in range(nc):
            w_x = half[i] + half_x[x + 1, i]
            w_x_before = half[i] + half_x[x - 1, i]
            w_y = half[i] + y_up(half[i])
            w_z = half[i] + jnp.where(is_last, half_up[i + 1], half_up[i])
            for c in range(COMP):
                up = jnp.where(is_last, turned[c][i + 1], turned[c][i])
                down = pltpu.roll(w_z * here[c][i], 1, 1)
                total = w_x * vel[c, x + 1, i] + w_x_before * vel[c, x - 1, i]
                total = total + w_y * y_up(here[c][i]) + y_down(w_y * here[c][i])
                total = total + w_z * up + jnp.where(is_first, last[c], down)
                last[c] = down
                emit(c, i, here[c][i], total)

    def sweep(source, target, reach, unroll):
        def step(x, carry):
            def emit(c, i, here, beside):
                added = inv_x[x, i] * (rhs_x[c, x, i] + beside)
                target[c, x, i] = 0.2 * here + added

            stencil(source, x, emit)
            return carry

        lax.fori_loop(X0 - reach, X0 + nx + reach, step, 0, unroll=unroll)

    sweep(vel_a, vel_b, 2, 10)
    sweep(vel_b, vel_a, 1, 9)

    in_high = lax.broadcasted_iota(jnp.int32, (HIGH, LANES), 0)
    label = lax.broadcasted_iota(jnp.int32, (LOW, LANES), 0).astype(F32)
    label = label.astype(jnp.bfloat16).reshape(LOW // 16, 16, LANES)
    ones, zeros = jnp.ones_like(label), jnp.zeros_like(label)

    def gather(x, total):
        def split(t, i, value):
            top = value.astype(jnp.bfloat16).astype(F32)
            terms[2 * t, i] = top
            terms[2 * t + 1, i] = value - top

        def emit(c, i, here, beside):
            vel_out[c, x - X0, :, i * LANES : (i + 1) * LANES] = here[Y0 : Y0 + ny]
            split(c, i, rhs_x[c, x, i] - (diag_s[x, i] * here - beside))

        stencil(vel_a, x, emit)
        for i in range(nc):
            split(COMP, i, diag_s[x, i])
        for i in range(nc):
            ident = ids[x - X0, :, i * LANES : (i + 1) * LANES]
            low_s[i] = (ident % LOW).astype(F32)
            high_s[i] = ident // LOW
        for y in range(ny):
            left, right = [], []
            row, at = pl.ds(y, 1), pl.ds(Y0 + y, 1)
            for i in range(nc):
                mask = high_s[i, row] == in_high
                parts = [jnp.where(mask, terms[t, i, at], 0.0) for t in range(2 * (COMP + 1))]
                left.append(jnp.concatenate(parts, axis=0).astype(jnp.bfloat16))
                low = jnp.broadcast_to(low_s[i, row], (16, LANES)).astype(jnp.bfloat16)
                hot = jnp.where(low[None] == label, ones, zeros)
                right.append(hot.reshape(LOW, LANES))
            total = total + lax.dot_general(
                jnp.concatenate(left, axis=1),
                jnp.concatenate(right, axis=1),
                (((1,), (1,)), ((), ())),
                preferred_element_type=F32,
            )
        return total

    width = 2 * (COMP + 1) * HIGH
    total = lax.fori_loop(X0, X0 + nx, gather, jnp.zeros((width, LOW), F32), unroll=4)
    for t in range(COMP + 1):
        at = 2 * HIGH * t
        both = total[at : at + HIGH] + total[at + HIGH : at + 2 * HIGH]
        sums[pl.ds(HIGH * t, HIGH), pl.ds(0, LOW)] = both
    half = SUM_ROWS
    even = sums[pl.ds(0, half, stride=2)]
    odd = sums[pl.ds(1, half, stride=2)]
    lane = lax.broadcasted_iota(jnp.int32, even.shape, 1)
    packet = jnp.where(lane < LOW, even, pltpu.roll(odd, LOW, 1))
    mine = jnp.full((8, LANES), owner[0, 0], jnp.int32).astype(F32)
    for peer in range(packets.shape[0]):
        packets[peer, pl.ds(0, SUM_ROWS)] = packet
        packets[peer, pl.ds(SUM_ROWS, 8)] = mine


def swapped(value, bit):
    row = lax.broadcasted_iota(jnp.int32, value.shape, 0)
    after = pltpu.roll(value, GROUP - bit, 0)
    before = pltpu.roll(value, bit, 0)
    return jnp.where((row & bit) == 0, after, before)


def coarse_kernel(place, arrived, out, levels):
    peers, rows, _ = arrived.shape
    flat = arrived.reshape(peers * rows, LANES)
    owner = flat[pl.ds(rows - 8, peers, stride=rows)]
    lane = lax.broadcasted_iota(jnp.int32, owner.shape, 1)
    base = place[0] - place[0] % GROUP
    chosen = jnp.where(owner == (base + lane).astype(F32), 1.0, 0.0)[:, :GROUP]
    blocks = []
    for r in range(SUM_ROWS):
        blocks.append(flat[pl.ds(r, peers, stride=rows)])
    gathered = jnp.concatenate(blocks, axis=1)
    owned = lax.dot_general(
        chosen, gathered, (((0,), (0,)), ((), ())),
        precision=lax.Precision.HIGHEST, preferred_element_type=F32,
    )
    resid = [owned[:, c * NAGG : (c + 1) * NAGG] for c in range(COMP)]
    diag = 1.0 + owned[:, COMP * NAGG :]
    at = lax.broadcasted_iota(jnp.int32, diag.shape, 1)
    for level in range(MERGES + 1):
        coupling = 0.2 * jnp.minimum(diag, pltpu.roll(diag, NAGG - 1, 1))
        coupling = jnp.where(at == NAGG - 1, 0.0, coupling)

        def apply(vector):
            upper = coupling * pltpu.roll(vector, NAGG - 1, 1)
            lower = pltpu.roll(coupling * vector, 1, 1)
            return diag * vector - (upper + lower)

        left = []
        for c in range(COMP):
            correction = 0.8 * resid[c] / diag
            correction = correction + 0.8 * (resid[c] - apply(correction)) / diag
            levels[level, c] = correction
            out[c, pl.ds(level, 1)] = levels[level, c, pl.ds(place[0] % GROUP, 1)]
            if level < MERGES:
                rest = resid[c] - apply(correction)
                left.append(rest + swapped(rest, 2**level))
        if level < MERGES:
            resid = left
            diag = diag + swapped(diag, 2**level)


def shift(axis, value, by):
    count = lax.axis_size(axis)
    pairs = [(i, i + by) for i in range(count) if 0 <= i + by < count]
    return lax.ppermute(value, axis, pairs)


def shards(right_side, viscosity, reaction, agg_ids, owner_map):
    nx, ny, nz = viscosity.shape
    nc = nz // LANES
    width = lax.axis_size("gx")
    place = lax.axis_index("gx").astype(jnp.int32).reshape(1)
    smem = pl.BlockSpec(memory_space=pltpu.SMEM)
    vmem = pl.BlockSpec(memory_space=pltpu.VMEM)
    small = pltpu.CompilerParams(vmem_limit_bytes=SMALL)

    def face(at_high):
        first = jnp.where(at_high, nx - WIDE, 0)
        first_v = jnp.where(at_high, nx - VWIDE, 0)
        return jnp.concatenate(
            [
                lax.dynamic_slice_in_dim(right_side, first, WIDE, axis=1).reshape(-1, ny, nz),
                lax.dynamic_slice_in_dim(viscosity, first_v, VWIDE, axis=0),
                lax.dynamic_slice_in_dim(reaction, first, WIDE, axis=0),
            ],
            axis=0,
        )

    even = place[0] % 2 == 0
    to_far, to_near = face(jnp.logical_not(even)), face(even)
    beyond = [(i, i - 1 if i % 2 == 0 else i + 1) for i in range(width)]
    beyond = [(i, k) for i, k in beyond if 0 <= k < width]
    far = lax.ppermute(to_far, "gx", beyond)
    near = lax.ppermute(to_near, "gx", [(i, i ^ 1) for i in range(width)])
    y_message = jax.ShapeDtypeStruct((nx, ROWS, nz), F32)
    to_y_low, to_y_high = pl.pallas_call(
        pack_y,
        out_shape=(y_message, y_message),
        compiler_params=small,
        name="pack_y",
    )(right_side, viscosity, reaction)
    y_low = shift("gy", to_y_high, 1)
    y_high = shift("gy", to_y_low, -1)
    corner = jax.ShapeDtypeStruct((2, 24, nz), F32)
    to_c_low, to_c_high = pl.pallas_call(
        pack_corners,
        out_shape=(corner, corner),
        in_specs=[smem, vmem, vmem],
        compiler_params=small,
        name="pack_corners",
    )(place, near, far)
    c_low = shift("gy", to_c_high, 1)
    c_high = shift("gy", to_c_low, -1)

    wide = (nx + 2 * X0, nc, ny + 2 * Y0, LANES)
    velocity, packets = pl.pallas_call(
        fine_kernel,
        out_shape=(
            jax.ShapeDtypeStruct(right_side.shape, F32),
            jax.ShapeDtypeStruct((width, SUM_ROWS + 8, LANES), F32),
        ),
        in_specs=[smem, smem] + [vmem] * 10,
        scratch_shapes=[
            pltpu.VMEM(wide, F32),
            pltpu.VMEM(wide, F32),
            pltpu.VMEM((COMP,) + wide, F32),
            pltpu.VMEM(wide, F32),
            pltpu.VMEM((COMP,) + wide, F32),
            pltpu.VMEM((COMP,) + wide, F32),
            pltpu.VMEM(wide, F32),
            pltpu.VMEM((2 * (COMP + 1),) + wide[1:], F32),
            pltpu.VMEM((nc, ny, LANES), F32),
            pltpu.VMEM((nc, ny, LANES), jnp.int32),
            pltpu.VMEM((2 * SUM_ROWS, LANES), F32),
        ],
        compiler_params=pltpu.CompilerParams(vmem_limit_bytes=BIG),
        name="fine",
    )(
        place, owner_map, right_side, viscosity, reaction, agg_ids,
        near, far, y_low, y_high, c_low, c_high,
    )
    arrived = lax.all_to_all(packets, "gx", 0, 0, tiled=True)
    corrections = pl.pallas_call(
        coarse_kernel,
        out_shape=jax.ShapeDtypeStruct((COMP, MERGES + 1, NAGG), F32),
        in_specs=[smem, vmem],
        scratch_shapes=[pltpu.VMEM((MERGES + 1, COMP, GROUP, NAGG), F32)],
        compiler_params=small,
        name="coarse",
    )(place, arrived)
    return (velocity, corrections.transpose(1, 0, 2)[None, None])


def solution(mesh):
    return jax.shard_map(
        shards,
        mesh=mesh,
        in_specs=(
            P(None, "gx", "gy", None),
            P("gx", "gy", None),
            P("gx", "gy", None),
            P("gx", "gy", None),
            P("gx", "gy"),
        ),
        out_specs=(P(None, "gx", "gy", None), P("gx", "gy", None, None, None)),
        check_vma=False,
    )
```

time: 72.5 us -> 68 us (0.938)
  blocking collectives: 0 us -> 19 us
  waiting for transfers between devices: 18.6 us -> 7.95 us
  starting transfers between devices: 27.7 us -> 19.2 us
  Pallas kernels: 21 us -> 17.8 us
  local copies, waits for them, and re-layouts: 3.5 us -> 2.17 us
    all_to_all x0 -> x1, blocking collectives: none -> 19 us  [shards(): arrived = lax.all_to_all(packets, 'gx', 0, 0, tiled=True)]
    all_to_all x1 -> x0, waiting for transfers between devices: 10.2 us -> none  [shards(): arrived = lax.all_to_all(packets, 'gx', 0, 0, tiled=True)]
    all_to_all x1 -> x0, starting transfers between devices: 8.6 us -> none  [shards(): arrived = lax.all_to_all(packets, 'gx', 0, 0, tiled=True)]
    ppermute x0 -> x2, starting transfers between devices: none -> 5.86 us  [the longest x1 3.15 us: shards(): far = lax.ppermute(to_far, 'gx', beyond)]
    ppermute x6 -> x4, starting transfers between devices: 19.1 us -> 13.4 us  [shift(): return lax.ppermute(value, axis, pairs)]
    unnamed x14 -> x8, local copies, waits for them, and re-layouts: 3.5 us -> 0.02 us
    pallas_call x1, Pallas kernels: 18.2 us -> 15.8 us  [shards(): pl.pallas_call(fine_kernel, out_shape=(jax.ShapeDtypeStruct(right_side.sh...]
    dynamic_slice x0 -> x3, local copies, waits for them, and re-layouts: none -> 2.15 us  [the longest x1 1.11 us: face(): lax.dynamic_slice_in_dim(right_side, first, WIDE, axis=1)]
  transfers between devices with their start and end apart: 7 -> 6, of which waited for: 4 -> 4; matrix products, arithmetic and copies ran while one was open for 0% -> 0% of each run, Pallas kernels for 0% -> 1%
where the time goes in v3:
time: 68 us; the launch traced here: 67.7 us
  starting transfers between devices  19.2 us (28%)
  blocking collectives  19 us (28%)
  Pallas kernels  17.8 us (26%)
  waiting for transfers between devices  7.95 us (12%)
  local copies, waits for them, and re-layouts  2.17 us (3%)
  between operations  1.46 us (2%)
    all_to_all x1, blocking collectives, shards(): arrived = lax.all_to_all(packets, 'gx', 0, 0, tiled=True)  19 us
    pallas_call x1, Pallas kernels, shards(): pl.pallas_call(fine_kernel, out_shape=(jax.ShapeDtypeStruct(right_side.sh...  15.8 us
    ppermute x4, starting transfers between devices, shift(): return lax.ppermute(value, axis, pairs)  13.4 us
    ppermute x4, waiting for transfers between devices, shift(): return lax.ppermute(value, axis, pairs)  7.2 us
    ppermute x1, starting transfers between devices, shards(): far = lax.ppermute(to_far, 'gx', beyond)  3.15 us
    ppermute x1, starting transfers between devices, shards(): near = lax.ppermute(to_near, 'gx', [(i, i ^ 1) for i in range(width)])  2.72 us
    pallas_call x1, Pallas kernels, shards(): pl.pallas_call(coarse_kernel, out_shape=jax.ShapeDtypeStruct((COMP, MERGE...  1.67 us
  transfers between devices with their start and end apart: 6, of which 4 were waited for; matrix products, arithmetic and copies ran while one was open for 0% of the time, Pallas kernels for 1%

profile of v3, /device:TPU:225, one launch (start us, length us, event | category | flops | bytes accessed | tf_op | source)
XLA Modules:
  0.0 67.7 jit_solution(17627116234354057162)
XLA Ops:
  0.6 0.0 copy-start.1
  0.7 1.0 %constant_dynamic-slice_fusion = (f32[3,16,512]{2,1,0:T(8,128)S(1)}, f32[3,16,512]{2,1,0:T(8,128)S(1)}) fusion(f32[16,16,512]{2,1,0:T(8,128)} %react.3, s32[]{:T(128)S(6)} %select_n.29, s32[]{:T(128)S(6)} %select_n.27), kind=kLoop, calls=%fused_computation.2 | loop fusion | bytes 393224 | tf_op jit(solution)/shard_map/dynamic_slice | solution.py:332
  1.7 1.1 %constant_dynamic-slice_fusion.2 = (f32[3,3,16,512]{3,2,1,0:T(8,128)S(1)}, f32[3,3,16,512]{3,2,1,0:T(8,128)S(1)}) fusion(f32[3,16,16,512]{3,2,1,0:T(8,128)} %rhs.3, s32[]{:T(128)S(6)} %select_n.29, s32[]{:T(128)S(6)} %select_n.27), kind=kLoop, calls=%fused_computation.4 | loop fusion | bytes 1179656 | tf_op jit(solution)/shard_map/dynamic_slice | solution.py:330
  2.8 0.0 copy-done.1
  2.8 0.0 copy-start
  2.8 0.0 copy-start.2
  2.9 2.7 %collective-permute-start = (f32[16,16,512]{2,1,0:T(8,128)S(1)}, f32[16,16,512]{2,1,0:T(8,128)S(1)}, u32[]{:S(2)}, u32[]{:S(2)}) collective-permute-start(f32[16,16,512]{2,1,0:T(8,128)S(1)} %pad_maximum_fusion), channel_id=1, source_target_pairs={{0,16},{16,0},{32,48},{48,32},{64,80},{80,64},{96,112},{112,96},{1... | collective-permute-start | bytes 1572872 | tf_op jit(solution)/shard_map/ppermute | solution.py:342
  5.7 0.0 copy-start.3
  5.7 3.1 %collective-permute-start.1 = (f32[16,16,512]{2,1,0:T(8,128)S(1)}, f32[16,16,512]{2,1,0:T(8,128)S(1)}, u32[]{:S(2)}, u32[]{:S(2)}) collective-permute-start(f32[16,16,512]{2,1,0:T(8,128)S(1)} %pad_maximum_fusion.1), channel_id=1, source_target_pairs={{16,32},{32,16},{48,64},{64,48},{80,96},{96,80},{112,128},{128,112... | collective-permute-start | bytes 1572872 | tf_op jit(solution)/shard_map/ppermute | solution.py:341
  8.9 0.0 copy-done
  8.9 0.0 copy-done.2
  8.9 0.3 pack_y.1
  9.2 4.8 %collective-permute-start.2 = (f32[16,16,512]{2,1,0:T(8,128)S(1)}, f32[16,16,512]{2,1,0:T(8,128)S(1)}, u32[]{:S(2)}, u32[]{:S(2)}) collective-permute-start(f32[16,16,512]{2,1,0:T(8,128)S(1)} %get-tuple-element.8), channel_id=1, source_target_pairs={{0,1},{1,2},{2,3},{3,4},{4,5},{5,6},{6,7},{7,8},{8,9},{9,10},{10,1... | collective-permute-start | bytes 1572872 | tf_op jit(solution)/shard_map/ppermute | solution.py:313
  13.9 1.9 %collective-permute-start.3 = (f32[16,16,512]{2,1,0:T(8,128)S(1)}, f32[16,16,512]{2,1,0:T(8,128)S(1)}, u32[]{:S(2)}, u32[]{:S(2)}) collective-permute-start(f32[16,16,512]{2,1,0:T(8,128)S(1)} %get-tuple-element.9), channel_id=1, source_target_pairs={{1,0},{2,1},{3,2},{4,3},{5,4},{6,5},{7,6},{8,7},{9,8},{10,9},{11,1... | collective-permute-start | bytes 1572872 | tf_op jit(solution)/shard_map/ppermute | solution.py:313
  15.9 0.0 collective-permute-done.near
  15.9 0.8 %collective-permute-done.1.far = f32[16,16,512]{2,1,0:T(8,128)S(1)} collective-permute-done((f32[16,16,512]{2,1,0:T(8,128)S(1)}, f32[16,16,512]{2,1,0:T(8,128)S(1)}, u32[]{:S(2)}, u32[]{:S(2)}) %collective-permute-start.1) | collective-permute-done | bytes 524320 | tf_op jit(solution)/shard_map/ppermute | solution.py:341
  16.6 0.1 pack_corners.1
  16.7 4.8 %collective-permute-start.4 = (f32[2,24,512]{2,1,0:T(8,128)S(1)}, f32[2,24,512]{2,1,0:T(8,128)S(1)}, u32[]{:S(2)}, u32[]{:S(2)}) collective-permute-start(f32[2,24,512]{2,1,0:T(8,128)S(1)} %get-tuple-element.10), channel_id=1, source_target_pairs={{0,1},{1,2},{2,3},{3,4},{4,5},{5,6},{6,7},{7,8},{8,9},{9,10},{10,1... | collective-permute-start | bytes 294920 | tf_op jit(solution)/shard_map/ppermute | solution.py:313
  21.5 1.9 %collective-permute-start.5 = (f32[2,24,512]{2,1,0:T(8,128)S(1)}, f32[2,24,512]{2,1,0:T(8,128)S(1)}, u32[]{:S(2)}, u32[]{:S(2)}) collective-permute-start(f32[2,24,512]{2,1,0:T(8,128)S(1)} %get-tuple-element.11), channel_id=1, source_target_pairs={{1,0},{2,1},{3,2},{4,3},{5,4},{6,5},{7,6},{8,7},{9,8},{10,9},{11,1... | collective-permute-start | bytes 294920 | tf_op jit(solution)/shard_map/ppermute | solution.py:313
  24.0 0.8 %collective-permute-done.2.y_low = f32[16,16,512]{2,1,0:T(8,128)S(1)} collective-permute-done((f32[16,16,512]{2,1,0:T(8,128)S(1)}, f32[16,16,512]{2,1,0:T(8,128)S(1)}, u32[]{:S(2)}, u32[]{:S(2)}) %collective-permute-start.2) | collective-permute-done | bytes 524320 | tf_op jit(solution)/shard_map/ppermute | solution.py:313
  24.9 5.3 %collective-permute-done.3.y_high = f32[16,16,512]{2,1,0:T(8,128)S(1)} collective-permute-done((f32[16,16,512]{2,1,0:T(8,128)S(1)}, f32[16,16,512]{2,1,0:T(8,128)S(1)}, u32[]{:S(2)}, u32[]{:S(2)}) %collective-permute-start.3) | collective-permute-done | bytes 524320 | tf_op jit(solution)/shard_map/ppermute | solution.py:313
  30.2 0.0 collective-permute-done.4.c_low
  30.2 1.0 %collective-permute-done.5.c_high = f32[2,24,512]{2,1,0:T(8,128)S(1)} collective-permute-done((f32[2,24,512]{2,1,0:T(8,128)S(1)}, f32[2,24,512]{2,1,0:T(8,128)S(1)}, u32[]{:S(2)}, u32[]{:S(2)}) %collective-permute-start.5) | collective-permute-done | bytes 98336 | tf_op jit(solution)/shard_map/ppermute | solution.py:313
  31.2 0.0 copy-done.3
  31.2 15.8 %fine.1 = (f32[3,16,16,512]{3,2,1,0:T(8,128)}, f32[32,24,128]{2,1,0:T(8,128)S(1)}) custom-call(s32[1]{0:T(128)} %bitcast.place, s32[1,1]{1,0:T(1,128)S(6)} %copy.7.owner, f32[3,16,16,512]{3,2,1,0:T(8,128)S(1)} %copy-done, f32[16,16,512]{2,1,0:T(8,128)S(1)} %copy-done.1, f32[16,16,512]{2,1,0:T(8,128)S(1)} %copy-done.2, s32[16,16,512]{2,1,0:T(8,128)S(1)} %copy-done.3, ...), custom_call_target="tpu_custom_call" | custom-call | tf_op jit(solution)/shard_map/fine/pallas_call | solution.py:364
  47.0 19.0 %all_to_all.5.arrived = f32[32,24,128]{2,1,0:T(8,128)S(1)} all-to-all(f32[32,24,128]{2,1,0:T(8,128)S(1)} %get-tuple-element.13), channel_id=1, replica_groups=mesh['gx'=32,'gy'=16] {'gx'}, dimensions={0} | all-to-all | bytes 786432 | tf_op jit(solution)/shard_map/all_to_all | solution.py:390
  66.0 1.7 %coarse.1 = f32[3,4,512]{2,1,0:T(4,128)} custom-call(s32[1]{0:T(128)} %bitcast.place, f32[32,24,128]{2,1,0:T(8,128)S(1)} %all_to_all.5.arrived), custom_call_target="tpu_custom_call" | custom-call | tf_op jit(solution)/shard_map/coarse/pallas_call | solution.py:391
  (3 shorter events, 0.1 us)
Async XLA Ops:
  0.6 2.2 %copy-start.1 = (f32[16,16,512]{2,1,0:T(8,128)S(1)}, f32[16,16,512]{2,1,0:T(8,128)}, u32[]{:S(2)}) copy-start(f32[16,16,512]{2,1,0:T(8,128)} %visc.3) | copy-start | bytes 1572868
  2.8 6.1 %copy-start = (f32[3,16,16,512]{3,2,1,0:T(8,128)S(1)}, f32[3,16,16,512]{3,2,1,0:T(8,128)}, u32[]{:S(2)}) copy-start(f32[3,16,16,512]{3,2,1,0:T(8,128)} %rhs.3) | copy-start | bytes 4718596
  2.8 6.1 %copy-start.2 = (f32[16,16,512]{2,1,0:T(8,128)S(1)}, f32[16,16,512]{2,1,0:T(8,128)}, u32[]{:S(2)}) copy-start(f32[16,16,512]{2,1,0:T(8,128)} %react.3) | copy-start | bytes 1572868
  2.9 13.0 %collective-permute-start = (f32[16,16,512]{2,1,0:T(8,128)S(1)}, f32[16,16,512]{2,1,0:T(8,128)S(1)}, u32[]{:S(2)}, u32[]{:S(2)}) collective-permute-start(f32[16,16,512]{2,1,0:T(8,128)S(1)} %pad_maximum_fusion), channel_id=1, source_target_pairs={{0,16},{16,0},{32,48},{48,32},{64,80},{80,64},{96,112},{112,96},{1... | collective-permute-start | bytes 1572872 | tf_op jit(solution)/shard_map/ppermute | solution.py:342
  5.7 25.5 %copy-start.3 = (s32[16,16,512]{2,1,0:T(8,128)S(1)}, s32[16,16,512]{2,1,0:T(8,128)}, u32[]{:S(2)}) copy-start(s32[16,16,512]{2,1,0:T(8,128)} %ids.1) | copy-start | bytes 1572868
  5.7 10.9 %collective-permute-start.1 = (f32[16,16,512]{2,1,0:T(8,128)S(1)}, f32[16,16,512]{2,1,0:T(8,128)S(1)}, u32[]{:S(2)}, u32[]{:S(2)}) collective-permute-start(f32[16,16,512]{2,1,0:T(8,128)S(1)} %pad_maximum_fusion.1), channel_id=1, source_target_pairs={{16,32},{32,16},{48,64},{64,48},{80,96},{96,80},{112,128},{128,112... | collective-permute-start | bytes 1572872 | tf_op jit(solution)/shard_map/ppermute | solution.py:341
  9.2 15.7 %collective-permute-start.2 = (f32[16,16,512]{2,1,0:T(8,128)S(1)}, f32[16,16,512]{2,1,0:T(8,128)S(1)}, u32[]{:S(2)}, u32[]{:S(2)}) collective-permute-start(f32[16,16,512]{2,1,0:T(8,128)S(1)} %get-tuple-element.8), channel_id=1, source_target_pairs={{0,1},{1,2},{2,3},{3,4},{4,5},{5,6},{6,7},{7,8},{8,9},{9,10},{10,1... | collective-permute-start | bytes 1572872 | tf_op jit(solution)/shard_map/ppermute | solution.py:313
  13.9 16.2 %collective-permute-start.3 = (f32[16,16,512]{2,1,0:T(8,128)S(1)}, f32[16,16,512]{2,1,0:T(8,128)S(1)}, u32[]{:S(2)}, u32[]{:S(2)}) collective-permute-start(f32[16,16,512]{2,1,0:T(8,128)S(1)} %get-tuple-element.9), channel_id=1, source_target_pairs={{1,0},{2,1},{3,2},{4,3},{5,4},{6,5},{7,6},{8,7},{9,8},{10,9},{11,1... | collective-permute-start | bytes 1572872 | tf_op jit(solution)/shard_map/ppermute | solution.py:313
  16.7 13.5 %collective-permute-start.4 = (f32[2,24,512]{2,1,0:T(8,128)S(1)}, f32[2,24,512]{2,1,0:T(8,128)S(1)}, u32[]{:S(2)}, u32[]{:S(2)}) collective-permute-start(f32[2,24,512]{2,1,0:T(8,128)S(1)} %get-tuple-element.10), channel_id=1, source_target_pairs={{0,1},{1,2},{2,3},{3,4},{4,5},{5,6},{6,7},{7,8},{8,9},{9,10},{10,1... | collective-permute-start | bytes 294920 | tf_op jit(solution)/shard_map/ppermute | solution.py:313
  21.5 9.8 %collective-permute-start.5 = (f32[2,24,512]{2,1,0:T(8,128)S(1)}, f32[2,24,512]{2,1,0:T(8,128)S(1)}, u32[]{:S(2)}, u32[]{:S(2)}) collective-permute-start(f32[2,24,512]{2,1,0:T(8,128)S(1)} %get-tuple-element.11), channel_id=1, source_target_pairs={{1,0},{2,1},{3,2},{4,3},{5,4},{6,5},{7,6},{8,7},{9,8},{10,9},{11,1... | collective-permute-start | bytes 294920 | tf_op jit(solution)/shard_map/ppermute | solution.py:313

commit v4 on v3

--- a/solution.py
+++ b/solution.py
@@ -15,6 +15,10 @@
 VISC_AT = COMP * WIDE
 REACT_AT = VISC_AT + VWIDE
 ROWS = REACT_AT + WIDE
+Y_VISC_AT = COMP * WIDE
+Y_REACT_AT = Y_VISC_AT + WIDE
+Y_ROWS = Y_REACT_AT + WIDE
+CORNER = 18
 X0 = VWIDE
 Y0 = VWIDE
 F32 = jnp.float32
@@ -27,7 +31,7 @@
 
 def corner_rows():
     table = []
-    for away, at in ((1, 0), (2, 16), (3, 22)):
+    for away, at in ((1, 0), (2, 11), (3, 17)):
         left = WIDE - away
         if left:
             for c in range(COMP):
@@ -43,16 +47,21 @@
 def pack_y(rhs, visc, react, y_low, y_high):
     nx, ny, _ = visc.shape
     for x in range(nx):
+        at = x * Y_ROWS
         for c in range(COMP):
-            rows = pl.ds(c * WIDE, WIDE)
-            y_low[x, rows] = rhs[c, x, pl.ds(0, WIDE)]
-            y_high[x, rows] = rhs[c, x, pl.ds(ny - WIDE, WIDE)]
-        rows = pl.ds(VISC_AT, VWIDE)
-        y_low[x, rows] = visc[x, pl.ds(0, VWIDE)]
-        y_high[x, rows] = visc[x, pl.ds(ny - VWIDE, VWIDE)]
-        rows = pl.ds(REACT_AT, WIDE)
-        y_low[x, rows] = react[x, pl.ds(0, WIDE)]
-        y_high[x, rows] = react[x, pl.ds(ny - WIDE, WIDE)]
+            rows = pl.ds(at + c * WIDE, WIDE)
+            y_low[rows] = rhs[c, x, pl.ds(0, WIDE)]
+            y_high[rows] = rhs[c, x, pl.ds(ny - WIDE, WIDE)]
+        rows = pl.ds(at + Y_VISC_AT, WIDE)
+        y_low[rows] = visc[x, pl.ds(0, WIDE)]
+        y_high[rows] = visc[x, pl.ds(ny - WIDE, WIDE)]
+        at = at + Y_REACT_AT
+        y_low[pl.ds(at, WIDE - 1)] = react[x, pl.ds(0, WIDE - 1)]
+        last = react[x, pl.ds(WIDE - 1, 1)] + 0.5 * visc[x, pl.ds(WIDE, 1)]
+        y_low[pl.ds(at + WIDE - 1, 1)] = last
+        last = react[x, pl.ds(ny - WIDE, 1)] + 0.5 * visc[x, pl.ds(ny - WIDE - 1, 1)]
+        y_high[pl.ds(at, 1)] = last
+        y_high[pl.ds(at + 1, WIDE - 1)] = react[x, pl.ds(ny - WIDE + 1, WIDE - 1)]
 
 
 def pack_corners(place, near, far, c_low, c_high):
@@ -63,9 +72,9 @@
             width = VWIDE if kind == "visc" else WIDE
             first = {"rhs": c * WIDE, "visc": VISC_AT, "react": REACT_AT}[kind]
             index = first + jnp.where(at_high, away - 1, width - away)
-            rows = pl.ds(at, count)
-            c_low[side, rows] = source[index, pl.ds(0, count)]
-            c_high[side, rows] = source[index, pl.ds(ny - count, count)]
+            rows = pl.ds(side * CORNER + at, count)
+            c_low[rows] = source[index, pl.ds(0, count)]
+            c_high[rows] = source[index, pl.ds(ny - count, count)]
 
 
 def chunks_of(value):
@@ -88,7 +97,7 @@
 def fine_kernel(
     place, owner, rhs, visc, react, ids, near, far, y_low, y_high, c_low, c_high,
     vel_out, packets,
-    half_x, react_x, rhs_x, inv_x, vel_a, vel_b, diag_s, terms, low_s, high_s, sums,
+    half_x, react_x, rhs_x, inv_x, vel_a, vel_b, diag_s, terms, low_s, high_s, sums, vel_s, sems,
 ):
     nx, ny, nz = visc.shape
     nc = nz // LANES
@@ -104,23 +113,25 @@
 
     own = pl.ds(Y0, ny)
 
-    def fill(x, carry):
+    before, after = pl.ds(Y0 - WIDE, WIDE), pl.ds(Y0 + ny, WIDE)
+    nothing = jnp.zeros((1, nz), F32)
+    for x in range(nx):
+        at = x * Y_ROWS
         for c in range(COMP):
             put("rhs", c, x + X0, own, rhs[c, x])
-            at = pl.ds(c * WIDE, WIDE)
-            put("rhs", c, x + X0, pl.ds(Y0 - WIDE, WIDE), y_low[x, at])
-            put("rhs", c, x + X0, pl.ds(Y0 + ny, WIDE), y_high[x, at])
+            rows = pl.ds(at + c * WIDE, WIDE)
+            put("rhs", c, x + X0, before, y_low[rows])
+            put("rhs", c, x + X0, after, y_high[rows])
         put("visc", 0, x + X0, own, visc[x])
-        at = pl.ds(VISC_AT, VWIDE)
-        put("visc", 0, x + X0, pl.ds(Y0 - VWIDE, VWIDE), y_low[x, at])
-        put("visc", 0, x + X0, pl.ds(Y0 + ny, VWIDE), y_high[x, at])
+        rows = pl.ds(at + Y_VISC_AT, WIDE)
+        put("visc", 0, x + X0, before, y_low[rows])
+        put("visc", 0, x + X0, after, y_high[rows])
+        put("visc", 0, x + X0, pl.ds(Y0 - VWIDE, 1), nothing)
+        put("visc", 0, x + X0, pl.ds(Y0 + ny + WIDE, 1), nothing)
         put("react", 0, x + X0, own, react[x])
-        at = pl.ds(REACT_AT, WIDE)
-        put("react", 0, x + X0, pl.ds(Y0 - WIDE, WIDE), y_low[x, at])
-        put("react", 0, x + X0, pl.ds(Y0 + ny, WIDE), y_high[x, at])
-        return carry
-
-    lax.fori_loop(0, nx, fill, 0)
+        rows = pl.ds(at + Y_REACT_AT, WIDE)
+        put("react", 0, x + X0, before, y_low[rows])
+        put("react", 0, x + X0, after, y_high[rows])
     even = place[0] % 2 == 0
     for source, at_high in ((near, even), (far, jnp.logical_not(even))):
         for away in range(1, VWIDE + 1):
@@ -136,8 +147,9 @@
         for away, kind, c, at, count in corner_rows():
             before, after = pl.ds(Y0 - count, count), pl.ds(Y0 + ny, count)
             x = jnp.where(at_high, X0 + nx - 1 + away, X0 - away)
-            put(kind, c, x, before, c_low[side, pl.ds(at, count)])
-            put(kind, c, x, after, c_high[side, pl.ds(at, count)])
+            rows = pl.ds(side * CORNER + at, count)
+            put(kind, c, x, before, c_low[rows])
+            put(kind, c, x, after, c_high[rows])
 
     def y_up(value):
         return pltpu.roll(value, value.shape[0] - 1, 0)
@@ -162,7 +174,7 @@
                 vel_a[c, x, i] = inv * rhs_x[c, x, i]
         return carry
 
-    lax.fori_loop(X0 - WIDE, X0 + nx + WIDE, prepare, 0, unroll=11)
+    lax.fori_loop(X0 - WIDE, X0 + nx + WIDE, prepare, 0, unroll=True)
 
     def stencil(vel, x, emit):
         shape = half_x.shape[2:]
@@ -188,7 +200,7 @@
                 last[c] = down
                 emit(c, i, here[c][i], total)
 
-    def sweep(source, target, reach, unroll):
+    def sweep(source, target, reach):
         def step(x, carry):
             def emit(c, i, here, beside):
                 added = inv_x[x, i] * (rhs_x[c, x, i] + beside)
@@ -197,15 +209,18 @@
             stencil(source, x, emit)
             return carry
 
-        lax.fori_loop(X0 - reach, X0 + nx + reach, step, 0, unroll=unroll)
-
-    sweep(vel_a, vel_b, 2, 10)
-    sweep(vel_b, vel_a, 1, 9)
+        lax.fori_loop(X0 - reach, X0 + nx + reach, step, 0, unroll=True)
+
+    sweep(vel_a, vel_b, 2)
+    sweep(vel_b, vel_a, 1)
 
     in_high = lax.broadcasted_iota(jnp.int32, (HIGH, LANES), 0)
     label = lax.broadcasted_iota(jnp.int32, (LOW, LANES), 0).astype(F32)
     label = label.astype(jnp.bfloat16).reshape(LOW // 16, 16, LANES)
     ones, zeros = jnp.ones_like(label), jnp.zeros_like(label)
+
+    def leave(x):
+        return pltpu.make_async_copy(vel_s.at[:, x], vel_out.at[:, x], sems.at[x])
 
     def gather(x, total):
         def split(t, i, value):
@@ -214,10 +229,11 @@
             terms[2 * t + 1, i] = value - top
 
         def emit(c, i, here, beside):
-            vel_out[c, x - X0, :, i * LANES : (i + 1) * LANES] = here[Y0 : Y0 + ny]
+            vel_s[c, x - X0, :, i * LANES : (i + 1) * LANES] = here[Y0 : Y0 + ny]
             split(c, i, rhs_x[c, x, i] - (diag_s[x, i] * here - beside))
 
         stencil(vel_a, x, emit)
+        leave(x - X0).start()
         for i in range(nc):
             split(COMP, i, diag_s[x, i])
         for i in range(nc):
@@ -257,6 +273,8 @@
     for peer in range(packets.shape[0]):
         packets[peer, pl.ds(0, SUM_ROWS)] = packet
         packets[peer, pl.ds(SUM_ROWS, 8)] = mine
+    for x in range(nx):
+        leave(x).wait()
 
 
 def swapped(value, bit):
@@ -340,7 +358,7 @@
     beyond = [(i, k) for i, k in beyond if 0 <= k < width]
     far = lax.ppermute(to_far, "gx", beyond)
     near = lax.ppermute(to_near, "gx", [(i, i ^ 1) for i in range(width)])
-    y_message = jax.ShapeDtypeStruct((nx, ROWS, nz), F32)
+    y_message = jax.ShapeDtypeStruct((nx * Y_ROWS, nz), F32)
     to_y_low, to_y_high = pl.pallas_call(
         pack_y,
         out_shape=(y_message, y_message),
@@ -349,7 +367,7 @@
     )(right_side, viscosity, reaction)
     y_low = shift("gy", to_y_high, 1)
     y_high = shift("gy", to_y_low, -1)
-    corner = jax.ShapeDtypeStruct((2, 24, nz), F32)
+    corner = jax.ShapeDtypeStruct((40, nz), F32)
     to_c_low, to_c_high = pl.pallas_call(
         pack_corners,
         out_shape=(corner, corner),
@@ -368,6 +386,7 @@
             jax.ShapeDtypeStruct((width, SUM_ROWS + 8, LANES), F32),
         ),
         in_specs=[smem, smem] + [vmem] * 10,
+        out_specs=(pl.BlockSpec(memory_space=pl.ANY), vmem),
         scratch_shapes=[
             pltpu.VMEM(wide, F32),
             pltpu.VMEM(wide, F32),
@@ -380,6 +399,8 @@
             pltpu.VMEM((nc, ny, LANES), F32),
             pltpu.VMEM((nc, ny, LANES), jnp.int32),
             pltpu.VMEM((2 * SUM_ROWS, LANES), F32),
+            pltpu.VMEM(right_side.shape, F32),
+            pltpu.SemaphoreType.DMA((nx,)),
         ],
         compiler_params=pltpu.CompilerParams(vmem_limit_bytes=BIG),
         name="fine",

time: 68 us -> 66.6 us (0.979)
  waiting for transfers between devices: 7.95 us -> 6.89 us
    ppermute x4, waiting for transfers between devices: 7.2 us -> 6.17 us  [shift(): return lax.ppermute(value, axis, pairs)]
  transfers between devices with their start and end apart: 6 -> 6, of which waited for: 4 -> 3; matrix products, arithmetic and copies ran while one was open for 0% -> 0% of each run, Pallas kernels for 1% -> 1%
where the time goes in v4:
time: 66.6 us; the launch traced here: 66.2 us
  starting transfers between devices  19.2 us (29%)
  blocking collectives  19.1 us (29%)
  Pallas kernels  17.4 us (26%)
  waiting for transfers between devices  6.89 us (10%)
  local copies, waits for them, and re-layouts  2.17 us (3%)
  between operations  1.48 us (2%)
    all_to_all x1, blocking collectives, shards(): arrived = lax.all_to_all(packets, 'gx', 0, 0, tiled=True)  19.1 us
    pallas_call x1, Pallas kernels, shards(): pl.pallas_call(fine_kernel, out_shape=(jax.ShapeDtypeStruct(right_side.sh...  15.3 us
    ppermute x4, starting transfers between devices, shift(): return lax.ppermute(value, axis, pairs)  13.4 us
    ppermute x4, waiting for transfers between devices, shift(): return lax.ppermute(value, axis, pairs)  6.17 us
    ppermute x1, starting transfers between devices, shards(): far = lax.ppermute(to_far, 'gx', beyond)  3.15 us
    ppermute x1, starting transfers between devices, shards(): near = lax.ppermute(to_near, 'gx', [(i, i ^ 1) for i in range(width)])  2.72 us
    pallas_call x1, Pallas kernels, shards(): pl.pallas_call(coarse_kernel, out_shape=jax.ShapeDtypeStruct((COMP, MERGE...  1.67 us
  transfers between devices with their start and end apart: 6, of which 3 were waited for; matrix products, arithmetic and copies ran while one was open for 0% of the time, Pallas kernels for 1%

profile of v4, /device:TPU:225, one launch (start us, length us, event | category | flops | bytes accessed | tf_op | source)
XLA Modules:
  0.0 66.2 jit_solution(2097926406407858908)
XLA Ops:
  0.6 0.0 copy-start.1
  0.7 1.0 %constant_dynamic-slice_fusion = (f32[3,16,512]{2,1,0:T(8,128)S(1)}, f32[3,16,512]{2,1,0:T(8,128)S(1)}) fusion(f32[16,16,512]{2,1,0:T(8,128)} %react.3, s32[]{:T(128)S(6)} %select_n.29, s32[]{:T(128)S(6)} %select_n.27), kind=kLoop, calls=%fused_computation.2 | loop fusion | bytes 393224 | tf_op jit(solution)/shard_map/dynamic_slice | solution.py:350
  1.7 1.1 %constant_dynamic-slice_fusion.2 = (f32[3,3,16,512]{3,2,1,0:T(8,128)S(1)}, f32[3,3,16,512]{3,2,1,0:T(8,128)S(1)}) fusion(f32[3,16,16,512]{3,2,1,0:T(8,128)} %rhs.3, s32[]{:T(128)S(6)} %select_n.29, s32[]{:T(128)S(6)} %select_n.27), kind=kLoop, calls=%fused_computation.4 | loop fusion | bytes 1179656 | tf_op jit(solution)/shard_map/dynamic_slice | solution.py:348
  2.8 0.0 copy-done.1
  2.8 0.0 copy-start
  2.8 0.0 copy-start.2
  2.9 2.7 %collective-permute-start = (f32[16,16,512]{2,1,0:T(8,128)S(1)}, f32[16,16,512]{2,1,0:T(8,128)S(1)}, u32[]{:S(2)}, u32[]{:S(2)}) collective-permute-start(f32[16,16,512]{2,1,0:T(8,128)S(1)} %pad_maximum_fusion), channel_id=1, source_target_pairs={{0,16},{16,0},{32,48},{48,32},{64,80},{80,64},{96,112},{112,96},{1... | collective-permute-start | bytes 1572872 | tf_op jit(solution)/shard_map/ppermute | solution.py:360
  5.7 0.0 copy-start.3
  5.7 3.1 %collective-permute-start.1 = (f32[16,16,512]{2,1,0:T(8,128)S(1)}, f32[16,16,512]{2,1,0:T(8,128)S(1)}, u32[]{:S(2)}, u32[]{:S(2)}) collective-permute-start(f32[16,16,512]{2,1,0:T(8,128)S(1)} %pad_maximum_fusion.1), channel_id=1, source_target_pairs={{16,32},{32,16},{48,64},{64,48},{80,96},{96,80},{112,128},{128,112... | collective-permute-start | bytes 1572872 | tf_op jit(solution)/shard_map/ppermute | solution.py:359
  8.9 0.0 copy-done
  8.9 0.0 copy-done.2
  8.9 0.3 pack_y.1
  9.2 4.8 %collective-permute-start.2 = (f32[240,512]{1,0:T(8,128)S(1)}, f32[240,512]{1,0:T(8,128)S(1)}, u32[]{:S(2)}, u32[]{:S(2)}) collective-permute-start(f32[240,512]{1,0:T(8,128)S(1)} %get-tuple-element.8), channel_id=1, source_target_pairs={{0,1},{1,2},{2,3},{3,4},{4,5},{5,6},{6,7},{7,8},{8,9},{9,10},{10,1... | collective-permute-start | bytes 1474568 | tf_op jit(solution)/shard_map/ppermute | solution.py:331
  14.0 1.9 %collective-permute-start.3 = (f32[240,512]{1,0:T(8,128)S(1)}, f32[240,512]{1,0:T(8,128)S(1)}, u32[]{:S(2)}, u32[]{:S(2)}) collective-permute-start(f32[240,512]{1,0:T(8,128)S(1)} %get-tuple-element.9), channel_id=1, source_target_pairs={{1,0},{2,1},{3,2},{4,3},{5,4},{6,5},{7,6},{8,7},{9,8},{10,9},{11,1... | collective-permute-start | bytes 1474568 | tf_op jit(solution)/shard_map/ppermute | solution.py:331
  15.9 0.0 collective-permute-done.near
  15.9 0.7 %collective-permute-done.1.far = f32[16,16,512]{2,1,0:T(8,128)S(1)} collective-permute-done((f32[16,16,512]{2,1,0:T(8,128)S(1)}, f32[16,16,512]{2,1,0:T(8,128)S(1)}, u32[]{:S(2)}, u32[]{:S(2)}) %collective-permute-start.1) | collective-permute-done | bytes 524320 | tf_op jit(solution)/shard_map/ppermute | solution.py:359
  16.6 0.1 pack_corners.1
  16.7 4.8 %collective-permute-start.4 = (f32[40,512]{1,0:T(8,128)S(1)}, f32[40,512]{1,0:T(8,128)S(1)}, u32[]{:S(2)}, u32[]{:S(2)}) collective-permute-start(f32[40,512]{1,0:T(8,128)S(1)} %get-tuple-element.10), channel_id=1, source_target_pairs={{0,1},{1,2},{2,3},{3,4},{4,5},{5,6},{6,7},{7,8},{8,9},{9,10},{10,1... | collective-permute-start | bytes 245768 | tf_op jit(solution)/shard_map/ppermute | solution.py:331
  21.4 1.9 %collective-permute-start.5 = (f32[40,512]{1,0:T(8,128)S(1)}, f32[40,512]{1,0:T(8,128)S(1)}, u32[]{:S(2)}, u32[]{:S(2)}) collective-permute-start(f32[40,512]{1,0:T(8,128)S(1)} %get-tuple-element.11), channel_id=1, source_target_pairs={{1,0},{2,1},{3,2},{4,3},{5,4},{6,5},{7,6},{8,7},{9,8},{10,9},{11,1... | collective-permute-start | bytes 245768 | tf_op jit(solution)/shard_map/ppermute | solution.py:331
  24.0 0.0 collective-permute-done.2.y_low
  24.0 5.3 %collective-permute-done.3.y_high = f32[240,512]{1,0:T(8,128)S(1)} collective-permute-done((f32[240,512]{1,0:T(8,128)S(1)}, f32[240,512]{1,0:T(8,128)S(1)}, u32[]{:S(2)}, u32[]{:S(2)}) %collective-permute-start.3) | collective-permute-done | bytes 491552 | tf_op jit(solution)/shard_map/ppermute | solution.py:331
  29.3 0.0 collective-permute-done.4.c_low
  29.3 0.9 %collective-permute-done.5.c_high = f32[40,512]{1,0:T(8,128)S(1)} collective-permute-done((f32[40,512]{1,0:T(8,128)S(1)}, f32[40,512]{1,0:T(8,128)S(1)}, u32[]{:S(2)}, u32[]{:S(2)}) %collective-permute-start.5) | collective-permute-done | bytes 81952 | tf_op jit(solution)/shard_map/ppermute | solution.py:331
  30.2 0.0 copy-done.3
  30.2 15.3 %fine.1 = (f32[3,16,16,512]{3,2,1,0:T(8,128)}, f32[32,24,128]{2,1,0:T(8,128)S(1)}) custom-call(s32[1]{0:T(128)} %bitcast.place, s32[1,1]{1,0:T(1,128)S(6)} %copy.7.owner, f32[3,16,16,512]{3,2,1,0:T(8,128)S(1)} %copy-done, f32[16,16,512]{2,1,0:T(8,128)S(1)} %copy-done.1, f32[16,16,512]{2,1,0:T(8,128)S(1)} %copy-done.2, s32[16,16,512]{2,1,0:T(8,128)S(1)} %copy-done.3, ...), custom_call_target="tpu_custom_call" | custom-call | tf_op jit(solution)/shard_map/fine/pallas_call | solution.py:382
  45.5 19.1 %all_to_all.5.arrived = f32[32,24,128]{2,1,0:T(8,128)S(1)} all-to-all(f32[32,24,128]{2,1,0:T(8,128)S(1)} %get-tuple-element.13), channel_id=1, replica_groups=mesh['gx'=32,'gy'=16] {'gx'}, dimensions={0} | all-to-all | bytes 786432 | tf_op jit(solution)/shard_map/all_to_all | solution.py:411
  64.6 1.7 %coarse.1 = f32[3,4,512]{2,1,0:T(4,128)} custom-call(s32[1]{0:T(128)} %bitcast.place, f32[32,24,128]{2,1,0:T(8,128)S(1)} %all_to_all.5.arrived), custom_call_target="tpu_custom_call" | custom-call | tf_op jit(solution)/shard_map/coarse/pallas_call | solution.py:412
  (3 shorter events, 0.1 us)
Async XLA Ops:
  0.6 2.2 %copy-start.1 = (f32[16,16,512]{2,1,0:T(8,128)S(1)}, f32[16,16,512]{2,1,0:T(8,128)}, u32[]{:S(2)}) copy-start(f32[16,16,512]{2,1,0:T(8,128)} %visc.3) | copy-start | bytes 1572868
  2.8 6.1 %copy-start = (f32[3,16,16,512]{3,2,1,0:T(8,128)S(1)}, f32[3,16,16,512]{3,2,1,0:T(8,128)}, u32[]{:S(2)}) copy-start(f32[3,16,16,512]{3,2,1,0:T(8,128)} %rhs.3) | copy-start | bytes 4718596
  2.8 6.1 %copy-start.2 = (f32[16,16,512]{2,1,0:T(8,128)S(1)}, f32[16,16,512]{2,1,0:T(8,128)}, u32[]{:S(2)}) copy-start(f32[16,16,512]{2,1,0:T(8,128)} %react.3) | copy-start | bytes 1572868
  2.9 13.0 %collective-permute-start = (f32[16,16,512]{2,1,0:T(8,128)S(1)}, f32[16,16,512]{2,1,0:T(8,128)S(1)}, u32[]{:S(2)}, u32[]{:S(2)}) collective-permute-start(f32[16,16,512]{2,1,0:T(8,128)S(1)} %pad_maximum_fusion), channel_id=1, source_target_pairs={{0,16},{16,0},{32,48},{48,32},{64,80},{80,64},{96,112},{112,96},{1... | collective-permute-start | bytes 1572872 | tf_op jit(solution)/shard_map/ppermute | solution.py:360
  5.7 24.5 %copy-start.3 = (s32[16,16,512]{2,1,0:T(8,128)S(1)}, s32[16,16,512]{2,1,0:T(8,128)}, u32[]{:S(2)}) copy-start(s32[16,16,512]{2,1,0:T(8,128)} %ids.1) | copy-start | bytes 1572868
  5.7 10.9 %collective-permute-start.1 = (f32[16,16,512]{2,1,0:T(8,128)S(1)}, f32[16,16,512]{2,1,0:T(8,128)S(1)}, u32[]{:S(2)}, u32[]{:S(2)}) collective-permute-start(f32[16,16,512]{2,1,0:T(8,128)S(1)} %pad_maximum_fusion.1), channel_id=1, source_target_pairs={{16,32},{32,16},{48,64},{64,48},{80,96},{96,80},{112,128},{128,112... | collective-permute-start | bytes 1572872 | tf_op jit(solution)/shard_map/ppermute | solution.py:359
  9.2 14.8 %collective-permute-start.2 = (f32[240,512]{1,0:T(8,128)S(1)}, f32[240,512]{1,0:T(8,128)S(1)}, u32[]{:S(2)}, u32[]{:S(2)}) collective-permute-start(f32[240,512]{1,0:T(8,128)S(1)} %get-tuple-element.8), channel_id=1, source_target_pairs={{0,1},{1,2},{2,3},{3,4},{4,5},{5,6},{6,7},{7,8},{8,9},{9,10},{10,1... | collective-permute-start | bytes 1474568 | tf_op jit(solution)/shard_map/ppermute | solution.py:331
  14.0 15.4 %collective-permute-start.3 = (f32[240,512]{1,0:T(8,128)S(1)}, f32[240,512]{1,0:T(8,128)S(1)}, u32[]{:S(2)}, u32[]{:S(2)}) collective-permute-start(f32[240,512]{1,0:T(8,128)S(1)} %get-tuple-element.9), channel_id=1, source_target_pairs={{1,0},{2,1},{3,2},{4,3},{5,4},{6,5},{7,6},{8,7},{9,8},{10,9},{11,1... | collective-permute-start | bytes 1474568 | tf_op jit(solution)/shard_map/ppermute | solution.py:331
  16.7 12.6 %collective-permute-start.4 = (f32[40,512]{1,0:T(8,128)S(1)}, f32[40,512]{1,0:T(8,128)S(1)}, u32[]{:S(2)}, u32[]{:S(2)}) collective-permute-start(f32[40,512]{1,0:T(8,128)S(1)} %get-tuple-element.10), channel_id=1, source_target_pairs={{0,1},{1,2},{2,3},{3,4},{4,5},{5,6},{6,7},{7,8},{8,9},{9,10},{10,1... | collective-permute-start | bytes 245768 | tf_op jit(solution)/shard_map/ppermute | solution.py:331
  21.4 8.8 %collective-permute-start.5 = (f32[40,512]{1,0:T(8,128)S(1)}, f32[40,512]{1,0:T(8,128)S(1)}, u32[]{:S(2)}, u32[]{:S(2)}) collective-permute-start(f32[40,512]{1,0:T(8,128)S(1)} %get-tuple-element.11), channel_id=1, source_target_pairs={{1,0},{2,1},{3,2},{4,3},{5,4},{6,5},{7,6},{8,7},{9,8},{10,9},{11,1... | collective-permute-start | bytes 245768 | tf_op jit(solution)/shard_map/ppermute | solution.py:331

commit v5 on v4

--- a/solution.py
+++ b/solution.py
@@ -1,3 +1,5 @@
+import functools
+
 import jax
 import jax.numpy as jnp
 from jax import lax
@@ -44,7 +46,23 @@
     return table
 
 
-def pack_y(rhs, visc, react, y_low, y_high):
+def by_parity(place, act, *pairs):
+    even = place[0] % 2 == 0
+
+    @pl.when(even)
+    def _():
+        act(*[ref for first, second in pairs for ref in (second, first)])
+
+    @pl.when(jnp.logical_not(even))
+    def _():
+        act(*[ref for pair in pairs for ref in pair])
+
+
+def pack_y(place, rhs, visc, react, y_first, y_second):
+    by_parity(place, functools.partial(gy_faces, rhs, visc, react), (y_first, y_second))
+
+
+def gy_faces(rhs, visc, react, y_low, y_high):
     nx, ny, _ = visc.shape
     for x in range(nx):
         at = x * Y_ROWS
@@ -64,17 +82,21 @@
         y_high[pl.ds(at + 1, WIDE - 1)] = react[x, pl.ds(ny - WIDE + 1, WIDE - 1)]
 
 
-def pack_corners(place, near, far, c_low, c_high):
+def pack_corners(place, near, far, c_first, c_second):
+    even = place[0] % 2 == 0
     ny = near.shape[1]
-    even = place[0] % 2 == 0
-    for side, (source, at_high) in enumerate(((near, even), (far, jnp.logical_not(even)))):
-        for away, kind, c, at, count in corner_rows():
-            width = VWIDE if kind == "visc" else WIDE
-            first = {"rhs": c * WIDE, "visc": VISC_AT, "react": REACT_AT}[kind]
-            index = first + jnp.where(at_high, away - 1, width - away)
-            rows = pl.ds(side * CORNER + at, count)
-            c_low[rows] = source[index, pl.ds(0, count)]
-            c_high[rows] = source[index, pl.ds(ny - count, count)]
+
+    def fill(c_low, c_high):
+        for side, (source, at_high) in enumerate(((near, even), (far, jnp.logical_not(even)))):
+            for away, kind, c, at, count in corner_rows():
+                width = VWIDE if kind == "visc" else WIDE
+                first = {"rhs": c * WIDE, "visc": VISC_AT, "react": REACT_AT}[kind]
+                index = first + jnp.where(at_high, away - 1, width - away)
+                rows = pl.ds(side * CORNER + at, count)
+                c_low[rows] = source[index, pl.ds(0, count)]
+                c_high[rows] = source[index, pl.ds(ny - count, count)]
+
+    by_parity(place, fill, (c_first, c_second))
 
 
 def chunks_of(value):
@@ -95,7 +117,7 @@
 
 
 def fine_kernel(
-    place, owner, rhs, visc, react, ids, near, far, y_low, y_high, c_low, c_high,
+    place, owner, rhs, visc, react, ids, near, far, y_first, y_second, c_first, c_second,
     vel_out, packets,
     half_x, react_x, rhs_x, inv_x, vel_a, vel_b, diag_s, terms, low_s, high_s, sums, vel_s, sems,
 ):
@@ -113,25 +135,14 @@
 
     own = pl.ds(Y0, ny)
 
-    before, after = pl.ds(Y0 - WIDE, WIDE), pl.ds(Y0 + ny, WIDE)
     nothing = jnp.zeros((1, nz), F32)
     for x in range(nx):
-        at = x * Y_ROWS
         for c in range(COMP):
             put("rhs", c, x + X0, own, rhs[c, x])
-            rows = pl.ds(at + c * WIDE, WIDE)
-            put("rhs", c, x + X0, before, y_low[rows])
-            put("rhs", c, x + X0, after, y_high[rows])
         put("visc", 0, x + X0, own, visc[x])
-        rows = pl.ds(at + Y_VISC_AT, WIDE)
-        put("visc", 0, x + X0, before, y_low[rows])
-        put("visc", 0, x + X0, after, y_high[rows])
         put("visc", 0, x + X0, pl.ds(Y0 - VWIDE, 1), nothing)
         put("visc", 0, x + X0, pl.ds(Y0 + ny + WIDE, 1), nothing)
         put("react", 0, x + X0, own, react[x])
-        rows = pl.ds(at + Y_REACT_AT, WIDE)
-        put("react", 0, x + X0, before, y_low[rows])
-        put("react", 0, x + X0, after, y_high[rows])
     even = place[0] % 2 == 0
     for source, at_high in ((near, even), (far, jnp.logical_not(even))):
         for away in range(1, VWIDE + 1):
@@ -143,13 +154,30 @@
                 for c in range(COMP):
                     put("rhs", c, x, own, source[c * WIDE + place_w])
                 put("react", 0, x, own, source[REACT_AT + place_w])
-    for side, at_high in enumerate((even, jnp.logical_not(even))):
-        for away, kind, c, at, count in corner_rows():
-            before, after = pl.ds(Y0 - count, count), pl.ds(Y0 + ny, count)
-            x = jnp.where(at_high, X0 + nx - 1 + away, X0 - away)
-            rows = pl.ds(side * CORNER + at, count)
-            put(kind, c, x, before, c_low[rows])
-            put(kind, c, x, after, c_high[rows])
+
+    def fill_y(y_high, y_low, c_high, c_low):
+        before, after = pl.ds(Y0 - WIDE, WIDE), pl.ds(Y0 + ny, WIDE)
+        for x in range(nx):
+            at = x * Y_ROWS
+            for c in range(COMP):
+                rows = pl.ds(at + c * WIDE, WIDE)
+                put("rhs", c, x + X0, before, y_low[rows])
+                put("rhs", c, x + X0, after, y_high[rows])
+            rows = pl.ds(at + Y_VISC_AT, WIDE)
+            put("visc", 0, x + X0, before, y_low[rows])
+            put("visc", 0, x + X0, after, y_high[rows])
+            rows = pl.ds(at + Y_REACT_AT, WIDE)
+            put("react", 0, x + X0, before, y_low[rows])
+            put("react", 0, x + X0, after, y_high[rows])
+        for side, at_high in enumerate((even, jnp.logical_not(even))):
+            for away, kind, c, at, count in corner_rows():
+                before, after = pl.ds(Y0 - count, count), pl.ds(Y0 + ny, count)
+                x = jnp.where(at_high, X0 + nx - 1 + away, X0 - away)
+                rows = pl.ds(side * CORNER + at, count)
+                put(kind, c, x, before, c_low[rows])
+                put(kind, c, x, after, c_high[rows])
+
+    by_parity(place, fill_y, (y_first, y_second), (c_first, c_second))
 
     def y_up(value):
         return pltpu.roll(value, value.shape[0] - 1, 0)
@@ -325,12 +353,6 @@
             diag = diag + swapped(diag, 2**level)
 
 
-def shift(axis, value, by):
-    count = lax.axis_size(axis)
-    pairs = [(i, i + by) for i in range(count) if 0 <= i + by < count]
-    return lax.ppermute(value, axis, pairs)
-
-
 def shards(right_side, viscosity, reaction, agg_ids, owner_map):
     nx, ny, nz = viscosity.shape
     nc = nz // LANES
@@ -359,24 +381,36 @@
     far = lax.ppermute(to_far, "gx", beyond)
     near = lax.ppermute(to_near, "gx", [(i, i ^ 1) for i in range(width)])
     y_message = jax.ShapeDtypeStruct((nx * Y_ROWS, nz), F32)
-    to_y_low, to_y_high = pl.pallas_call(
+    to_first, to_second = pl.pallas_call(
         pack_y,
         out_shape=(y_message, y_message),
+        in_specs=[smem, vmem, vmem, vmem],
         compiler_params=small,
         name="pack_y",
-    )(right_side, viscosity, reaction)
-    y_low = shift("gy", to_y_high, 1)
-    y_high = shift("gy", to_y_low, -1)
+    )(place, right_side, viscosity, reaction)
     corner = jax.ShapeDtypeStruct((40, nz), F32)
-    to_c_low, to_c_high = pl.pallas_call(
+    to_c_first, to_c_second = pl.pallas_call(
         pack_corners,
         out_shape=(corner, corner),
         in_specs=[smem, vmem, vmem],
         compiler_params=small,
         name="pack_corners",
     )(place, near, far)
-    c_low = shift("gy", to_c_high, 1)
-    c_high = shift("gy", to_c_low, -1)
+
+    def along_gy(value, by):
+        height = lax.axis_size("gy")
+        pairs = []
+        for i in range(width):
+            for j in range(height):
+                k = j + by if i % 2 == 0 else j - by
+                if 0 <= k < height:
+                    pairs.append((i * height + j, i * height + k))
+        return lax.ppermute(value, ("gx", "gy"), pairs)
+
+    y_first = along_gy(to_first, 1)
+    y_second = along_gy(to_second, -1)
+    c_first = along_gy(to_c_first, 1)
+    c_second = along_gy(to_c_second, -1)
 
     wide = (nx + 2 * X0, nc, ny + 2 * Y0, LANES)
     velocity, packets = pl.pallas_call(
@@ -406,7 +440,7 @@
         name="fine",
     )(
         place, owner_map, right_side, viscosity, reaction, agg_ids,
-        near, far, y_low, y_high, c_low, c_high,
+        near, far, y_first, y_second, c_first, c_second,
     )
     arrived = lax.all_to_all(packets, "gx", 0, 0, tiled=True)
     corrections = pl.pallas_call(

time: 66.6 us -> 63.2 us (0.949)
  waiting for transfers between devices: 6.89 us -> 1.58 us
  blocking collectives: 19.1 us -> 21.1 us
    ppermute x4, waiting for transfers between devices: 6.17 us -> 0.89 us  [along_gy(): return lax.ppermute(value, ('gx', 'gy'), pairs)]
    all_to_all x1, blocking collectives: 19.1 us -> 21.1 us  [shards(): arrived = lax.all_to_all(packets, 'gx', 0, 0, tiled=True)]
where the time goes in v5:
time: 63.2 us; the launch traced here: 62.8 us
  blocking collectives  21.1 us (33%)
  starting transfers between devices  19.1 us (30%)
  Pallas kernels  17.3 us (27%)
  local copies, waits for them, and re-layouts  2.17 us (3%)
  waiting for transfers between devices  1.58 us (2%)
  between operations  1.48 us (2%)
    all_to_all x1, blocking collectives, shards(): arrived = lax.all_to_all(packets, 'gx', 0, 0, tiled=True)  21.1 us
    pallas_call x1, Pallas kernels, shards(): pl.pallas_call(fine_kernel, out_shape=(jax.ShapeDtypeStruct(right_side.sh...  15.2 us
    ppermute x4, starting transfers between devices, along_gy(): return lax.ppermute(value, ('gx', 'gy'), pairs)  13.4 us
    ppermute x1, starting transfers between devices, shards(): far = lax.ppermute(to_far, 'gx', beyond)  3.02 us
    ppermute x1, starting transfers between devices, shards(): near = lax.ppermute(to_near, 'gx', [(i, i ^ 1) for i in range(width)])  2.72 us
    pallas_call x1, Pallas kernels, shards(): pl.pallas_call(coarse_kernel, out_shape=jax.ShapeDtypeStruct((COMP, MERGE...  1.67 us
  transfers between devices with their start and end apart: 6, of which 3 were waited for; matrix products, arithmetic and copies ran while one was open for 0% of the time, Pallas kernels for 1%

profile of v5, /device:TPU:225, one launch (start us, length us, event | category | flops | bytes accessed | tf_op | source)
XLA Modules:
  0.0 62.8 jit_solution(4601172565571490687)
XLA Ops:
  0.6 0.0 copy-start.1
  0.7 1.0 %constant_dynamic-slice_fusion = (f32[3,16,512]{2,1,0:T(8,128)S(1)}, f32[3,16,512]{2,1,0:T(8,128)S(1)}) fusion(f32[16,16,512]{2,1,0:T(8,128)} %react.3, s32[]{:T(128)S(6)} %select_n.29, s32[]{:T(128)S(6)} %select_n.27), kind=kLoop, calls=%fused_computation.2 | loop fusion | bytes 393224 | tf_op jit(solution)/shard_map/dynamic_slice | solution.py:372
  1.7 1.1 %constant_dynamic-slice_fusion.2 = (f32[3,3,16,512]{3,2,1,0:T(8,128)S(1)}, f32[3,3,16,512]{3,2,1,0:T(8,128)S(1)}) fusion(f32[3,16,16,512]{3,2,1,0:T(8,128)} %rhs.3, s32[]{:T(128)S(6)} %select_n.29, s32[]{:T(128)S(6)} %select_n.27), kind=kLoop, calls=%fused_computation.4 | loop fusion | bytes 1179656 | tf_op jit(solution)/shard_map/dynamic_slice | solution.py:370
  2.8 0.0 copy-done.1
  2.8 0.0 copy-start
  2.8 0.0 copy-start.2
  2.9 2.7 %collective-permute-start = (f32[16,16,512]{2,1,0:T(8,128)S(1)}, f32[16,16,512]{2,1,0:T(8,128)S(1)}, u32[]{:S(2)}, u32[]{:S(2)}) collective-permute-start(f32[16,16,512]{2,1,0:T(8,128)S(1)} %pad_maximum_fusion), channel_id=1, source_target_pairs={{0,16},{16,0},{32,48},{48,32},{64,80},{80,64},{96,112},{112,96},{1... | collective-permute-start | bytes 1572872 | tf_op jit(solution)/shard_map/ppermute | solution.py:382
  5.7 3.0 %collective-permute-start.1 = (f32[16,16,512]{2,1,0:T(8,128)S(1)}, f32[16,16,512]{2,1,0:T(8,128)S(1)}, u32[]{:S(2)}, u32[]{:S(2)}) collective-permute-start(f32[16,16,512]{2,1,0:T(8,128)S(1)} %pad_maximum_fusion.1), channel_id=1, source_target_pairs={{16,32},{32,16},{48,64},{64,48},{80,96},{96,80},{112,128},{128,112... | collective-permute-start | bytes 1572872 | tf_op jit(solution)/shard_map/ppermute | solution.py:381
  8.7 0.0 copy-done
  8.7 0.0 copy-done.2
  8.7 0.0 copy-start.3
  8.7 0.3 pack_y.1
  9.1 1.9 %collective-permute-start.2 = (f32[240,512]{1,0:T(8,128)S(1)}, f32[240,512]{1,0:T(8,128)S(1)}, u32[]{:S(2)}, u32[]{:S(2)}) collective-permute-start(f32[240,512]{1,0:T(8,128)S(1)} %get-tuple-element.8), channel_id=1, source_target_pairs={{0,1},{1,2},{2,3},{3,4},{4,5},{5,6},{6,7},{7,8},{8,9},{9,10},{10,1... | collective-permute-start | bytes 1474568 | tf_op jit(solution)/shard_map/ppermute | solution.py:408
  11.0 4.8 %collective-permute-start.3 = (f32[240,512]{1,0:T(8,128)S(1)}, f32[240,512]{1,0:T(8,128)S(1)}, u32[]{:S(2)}, u32[]{:S(2)}) collective-permute-start(f32[240,512]{1,0:T(8,128)S(1)} %get-tuple-element.9), channel_id=1, source_target_pairs={{1,0},{2,1},{3,2},{4,3},{5,4},{6,5},{7,6},{8,7},{9,8},{10,9},{11,1... | collective-permute-start | bytes 1474568 | tf_op jit(solution)/shard_map/ppermute | solution.py:408
  15.8 0.0 collective-permute-done.near
  15.8 0.7 %collective-permute-done.1.far = f32[16,16,512]{2,1,0:T(8,128)S(1)} collective-permute-done((f32[16,16,512]{2,1,0:T(8,128)S(1)}, f32[16,16,512]{2,1,0:T(8,128)S(1)}, u32[]{:S(2)}, u32[]{:S(2)}) %collective-permute-start.1) | collective-permute-done | bytes 524320 | tf_op jit(solution)/shard_map/ppermute | solution.py:381
  16.5 0.1 pack_corners.1
  16.5 1.9 %collective-permute-start.4 = (f32[40,512]{1,0:T(8,128)S(1)}, f32[40,512]{1,0:T(8,128)S(1)}, u32[]{:S(2)}, u32[]{:S(2)}) collective-permute-start(f32[40,512]{1,0:T(8,128)S(1)} %get-tuple-element.10), channel_id=1, source_target_pairs={{0,1},{1,2},{2,3},{3,4},{4,5},{5,6},{6,7},{7,8},{8,9},{9,10},{10,1... | collective-permute-start | bytes 245768 | tf_op jit(solution)/shard_map/ppermute | solution.py:408
  18.5 4.8 %collective-permute-start.5 = (f32[40,512]{1,0:T(8,128)S(1)}, f32[40,512]{1,0:T(8,128)S(1)}, u32[]{:S(2)}, u32[]{:S(2)}) collective-permute-start(f32[40,512]{1,0:T(8,128)S(1)} %get-tuple-element.11), channel_id=1, source_target_pairs={{1,0},{2,1},{3,2},{4,3},{5,4},{6,5},{7,6},{8,7},{9,8},{10,9},{11,1... | collective-permute-start | bytes 245768 | tf_op jit(solution)/shard_map/ppermute | solution.py:408
  23.9 0.0 collective-permute-done.2.y_first
  23.9 0.0 collective-permute-done.3.y_second
  23.9 0.4 collective-permute-done.4.c_first
  24.3 0.5 collective-permute-done.5.c_second
  24.8 0.0 copy-done.3
  24.8 15.2 %fine.1 = (f32[3,16,16,512]{3,2,1,0:T(8,128)}, f32[32,24,128]{2,1,0:T(8,128)S(1)}) custom-call(s32[1]{0:T(128)} %bitcast.place, s32[1,1]{1,0:T(1,128)S(6)} %copy.7.owner, f32[3,16,16,512]{3,2,1,0:T(8,128)S(1)} %copy-done, f32[16,16,512]{2,1,0:T(8,128)S(1)} %copy-done.1, f32[16,16,512]{2,1,0:T(8,128)S(1)} %copy-done.2, s32[16,16,512]{2,1,0:T(8,128)S(1)} %copy-done.3, ...), custom_call_target="tpu_custom_call" | custom-call | tf_op jit(solution)/shard_map/fine/pallas_call | solution.py:416
  40.0 21.1 %all_to_all.5.arrived = f32[32,24,128]{2,1,0:T(8,128)S(1)} all-to-all(f32[32,24,128]{2,1,0:T(8,128)S(1)} %get-tuple-element.13), channel_id=1, replica_groups=mesh['gx'=32,'gy'=16] {'gx'}, dimensions={0} | all-to-all | bytes 786432 | tf_op jit(solution)/shard_map/all_to_all | solution.py:445
  61.2 1.7 %coarse.1 = f32[3,4,512]{2,1,0:T(4,128)} custom-call(s32[1]{0:T(128)} %bitcast.place, f32[32,24,128]{2,1,0:T(8,128)S(1)} %all_to_all.5.arrived), custom_call_target="tpu_custom_call" | custom-call | tf_op jit(solution)/shard_map/coarse/pallas_call | solution.py:446
  (3 shorter events, 0.1 us)
Async XLA Ops:
  0.6 2.2 %copy-start.1 = (f32[16,16,512]{2,1,0:T(8,128)S(1)}, f32[16,16,512]{2,1,0:T(8,128)}, u32[]{:S(2)}) copy-start(f32[16,16,512]{2,1,0:T(8,128)} %visc.3) | copy-start | bytes 1572868
  2.8 5.9 %copy-start = (f32[3,16,16,512]{3,2,1,0:T(8,128)S(1)}, f32[3,16,16,512]{3,2,1,0:T(8,128)}, u32[]{:S(2)}) copy-start(f32[3,16,16,512]{3,2,1,0:T(8,128)} %rhs.3) | copy-start | bytes 4718596
  2.8 5.9 %copy-start.2 = (f32[16,16,512]{2,1,0:T(8,128)S(1)}, f32[16,16,512]{2,1,0:T(8,128)}, u32[]{:S(2)}) copy-start(f32[16,16,512]{2,1,0:T(8,128)} %react.3) | copy-start | bytes 1572868
  2.9 12.9 %collective-permute-start = (f32[16,16,512]{2,1,0:T(8,128)S(1)}, f32[16,16,512]{2,1,0:T(8,128)S(1)}, u32[]{:S(2)}, u32[]{:S(2)}) collective-permute-start(f32[16,16,512]{2,1,0:T(8,128)S(1)} %pad_maximum_fusion), channel_id=1, source_target_pairs={{0,16},{16,0},{32,48},{48,32},{64,80},{80,64},{96,112},{112,96},{1... | collective-permute-start | bytes 1572872 | tf_op jit(solution)/shard_map/ppermute | solution.py:382
  5.7 10.8 %collective-permute-start.1 = (f32[16,16,512]{2,1,0:T(8,128)S(1)}, f32[16,16,512]{2,1,0:T(8,128)S(1)}, u32[]{:S(2)}, u32[]{:S(2)}) collective-permute-start(f32[16,16,512]{2,1,0:T(8,128)S(1)} %pad_maximum_fusion.1), channel_id=1, source_target_pairs={{16,32},{32,16},{48,64},{64,48},{80,96},{96,80},{112,128},{128,112... | collective-permute-start | bytes 1572872 | tf_op jit(solution)/shard_map/ppermute | solution.py:381
  8.7 16.0 %copy-start.3 = (s32[16,16,512]{2,1,0:T(8,128)S(1)}, s32[16,16,512]{2,1,0:T(8,128)}, u32[]{:S(2)}) copy-start(s32[16,16,512]{2,1,0:T(8,128)} %ids.1) | copy-start | bytes 1572868
  9.1 14.8 %collective-permute-start.2 = (f32[240,512]{1,0:T(8,128)S(1)}, f32[240,512]{1,0:T(8,128)S(1)}, u32[]{:S(2)}, u32[]{:S(2)}) collective-permute-start(f32[240,512]{1,0:T(8,128)S(1)} %get-tuple-element.8), channel_id=1, source_target_pairs={{0,1},{1,2},{2,3},{3,4},{4,5},{5,6},{6,7},{7,8},{8,9},{9,10},{10,1... | collective-permute-start | bytes 1474568 | tf_op jit(solution)/shard_map/ppermute | solution.py:408
  11.0 12.9 %collective-permute-start.3 = (f32[240,512]{1,0:T(8,128)S(1)}, f32[240,512]{1,0:T(8,128)S(1)}, u32[]{:S(2)}, u32[]{:S(2)}) collective-permute-start(f32[240,512]{1,0:T(8,128)S(1)} %get-tuple-element.9), channel_id=1, source_target_pairs={{1,0},{2,1},{3,2},{4,3},{5,4},{6,5},{7,6},{8,7},{9,8},{10,9},{11,1... | collective-permute-start | bytes 1474568 | tf_op jit(solution)/shard_map/ppermute | solution.py:408
  16.5 7.8 %collective-permute-start.4 = (f32[40,512]{1,0:T(8,128)S(1)}, f32[40,512]{1,0:T(8,128)S(1)}, u32[]{:S(2)}, u32[]{:S(2)}) collective-permute-start(f32[40,512]{1,0:T(8,128)S(1)} %get-tuple-element.10), channel_id=1, source_target_pairs={{0,1},{1,2},{2,3},{3,4},{4,5},{5,6},{6,7},{7,8},{8,9},{9,10},{10,1... | collective-permute-start | bytes 245768 | tf_op jit(solution)/shard_map/ppermute | solution.py:408
  18.5 6.3 %collective-permute-start.5 = (f32[40,512]{1,0:T(8,128)S(1)}, f32[40,512]{1,0:T(8,128)S(1)}, u32[]{:S(2)}, u32[]{:S(2)}) collective-permute-start(f32[40,512]{1,0:T(8,128)S(1)} %get-tuple-element.11), channel_id=1, source_target_pairs={{1,0},{2,1},{3,2},{4,3},{5,4},{6,5},{7,6},{8,7},{9,8},{10,9},{11,1... | collective-permute-start | bytes 245768 | tf_op jit(solution)/shard_map/ppermute | solution.py:408
